TPU v7x, 512 devices: a whole 4x8x8 slice. The times are simulated.
512 devices in a mesh: pool: 8 (over z), context: 32 (over x, y), tensor: 2 (over core).
Axes of the slice: x: 4, y: 8, z: 8, core: 2. Of those that a mesh axis runs over, the one named last changes fastest.
Arguments:
- cache: bfloat16 [8, 32, 16, 576], P('pool', 'context'), may hold values from -6 to 6
- hit_slots: int32 [8, 32], P('pool'), may hold values from 0 to 31, each once within a row
- prefix_blocks: int32 [8], P('pool'), may hold values from 10 to 32, as said below
- suffix_len: int32 [8], P('pool'), may hold values from 512 to 2048, as said below
- suffix_latent: bfloat16 [8, 2048, 576], P('pool', 'context')
- suffix_query: bfloat16 [8, 2048, 64, 576], P('pool', 'context', 'tensor')
- decode_hidden: bfloat16 [8, 2, 7168], P('pool'), may hold values from -6 to 6
- kv_down: bfloat16 [7168, 576], P(('context', 'tensor')), may hold values from -0.0625 to 0.0625
- kv_gain: float32 [512], replicated, may hold values from 0.1 to 1.9
- decode_query: bfloat16 [8, 2, 64, 576], P('pool', None, 'tensor')
Outputs:
- suffix_context: bfloat16 [8, 2048, 64, 512], P('pool', 'context', 'tensor')
- decode_context: bfloat16 [8, 2, 64, 512], P('pool', None, 'tensor')
- decode_latent: bfloat16 [8, 2, 576], P('pool')
Inputs may be any that keep to these rules, and one draw needn't show every extreme that they name: `prefix_blocks`: some request has all of its group's 32 slots as hits. `suffix_len`: some request has all 2048 suffix tokens valid.
All inputs are finite; a program needn't handle non-finite values.
Results may differ from a plain program's by a relative error of at most 0.03.
Values may be sent and summed in bfloat16 or wider, within the bound.
A program may use at most 128 MiB of HBM per device.

v0:
```python
import math

import jax
import jax.numpy as jnp
from jax import lax
from jax.sharding import PartitionSpec as P

SCALE = 192.0 ** (-0.5)
NEG = -1e30


def attend(state, queries, key_rows, allowed):
    running_max, running_sum, accum = state
    lat_width = accum.shape[-1]
    scores = (
        jnp.einsum("rhc,kc->rhk", queries, key_rows, preferred_element_type=jnp.float32) * SCALE
    )
    scores = jnp.where(allowed[:, None, :], scores, NEG)
    new_max = jnp.maximum(running_max, jnp.max(scores, axis=-1))
    rescale = jnp.exp(running_max - new_max)
    weights = jnp.where(allowed[:, None, :], jnp.exp(scores - new_max[..., None]), 0.0).astype(
        jnp.bfloat16
    )
    running_sum = running_sum * rescale + jnp.sum(weights.astype(jnp.float32), axis=-1)
    accum = accum * rescale[..., None] + jnp.einsum(
        "rhk,kc->rhc", weights, key_rows[:, :lat_width], preferred_element_type=jnp.float32
    )
    return (new_max, running_sum, accum)


def attend_blocks(state, queries, key_rows, allowed):
    key_count = key_rows.shape[0]
    span_size = math.gcd(key_count, 512)
    if span_size == key_count:
        return attend(state, queries, key_rows, allowed)
    block_count = key_count // span_size
    key_blocks = key_rows.reshape(block_count, span_size, key_rows.shape[1])
    allow_blocks = jnp.moveaxis(allowed.reshape(allowed.shape[0], block_count, span_size), 1, 0)

    def advance(carry, item):
        return (attend(carry, queries, item[0], item[1]), None)

    state, unused = lax.scan(advance, state, (key_blocks, allow_blocks))
    return state


def fresh_state(row_count, heads, lat_width):
    return (
        jnp.full((row_count, heads), NEG, jnp.float32),
        jnp.zeros((row_count, heads), jnp.float32),
        jnp.zeros((row_count, heads, lat_width), jnp.float32),
    )


def rotate_latent(raw, kv_gain, positions):
    lat_width = kv_gain.shape[0]
    latent = raw[:, :lat_width]
    normed = latent * lax.rsqrt(jnp.mean(latent * latent, axis=-1, keepdims=True) + 1e-06) * kv_gain
    half = (raw.shape[1] - lat_width) // 2
    freq = 10000.0 ** (-jnp.arange(half, dtype=jnp.float32) / half)
    angle = positions[:, None] * freq[None, :]
    first = raw[:, lat_width : lat_width + half]
    second = raw[:, lat_width + half :]
    cosine = jnp.cos(angle)
    sine = jnp.sin(angle)
    rotated = jnp.concatenate(
        [first * cosine - second * sine, second * cosine + first * sine], axis=-1
    )
    return jnp.concatenate([normed, rotated], axis=-1).astype(jnp.bfloat16)


def finish(state):
    return (state[2] / state[1][..., None]).astype(jnp.bfloat16)


def on_device(
    cache,
    hit_slots,
    prefix_blocks,
    suffix_len,
    suffix_latent,
    suffix_query,
    decode_hidden,
    kv_down,
    kv_gain,
    decode_query,
):
    lat_width = kv_gain.shape[0]
    slot_total = hit_slots.shape[1]
    block_rows = cache.shape[2]
    kv_width = cache.shape[3]
    ctx_rank = lax.axis_index("context")
    slot_ids = jnp.arange(slot_total, dtype=jnp.int32)
    slot_live = jnp.any(
        (hit_slots[0][:, None] == slot_ids[None, :]) & (slot_ids < prefix_blocks[0])[:, None],
        axis=0,
    )
    queries = suffix_query[0]
    tok_count = queries.shape[0]
    heads = queries.shape[1]
    tok_ids = ctx_rank * tok_count + jnp.arange(tok_count, dtype=jnp.int32)
    last_token = ctx_rank * tok_count + tok_count - 1
    dec_queries = decode_query[0]
    dec_count = dec_queries.shape[0]
    dec_ids = jnp.arange(dec_count, dtype=jnp.int32)
    suffix_end = suffix_len[0]
    row_count = kv_down.shape[0]
    part_index = lax.axis_index(("context", "tensor"))
    hidden_part = lax.dynamic_slice_in_dim(decode_hidden[0], part_index * row_count, row_count, 1)
    raw = lax.psum(
        jnp.dot(hidden_part, kv_down, preferred_element_type=jnp.float32), ("context", "tensor")
    )
    positions = (prefix_blocks[0] * block_rows + suffix_end + dec_ids).astype(jnp.float32)
    fresh = rotate_latent(raw, kv_gain, positions)
    states = (fresh_state(tok_count, heads, lat_width), fresh_state(dec_count, heads, lat_width))
    key_rows = lax.all_gather(suffix_latent, "context", axis=1, tiled=True)[0]
    key_count = key_rows.shape[0]
    key_ids = jnp.arange(key_count, dtype=jnp.int32)

    def visit(tok_carry):
        tok_allow = key_ids[None, :] <= tok_ids[:, None]
        return attend_blocks(tok_carry, queries, key_rows, tok_allow)

    def leave(tok_carry):
        return tok_carry

    tok_state = lax.cond(jnp.int32(0) <= last_token, visit, leave, states[0])
    dec_allow = jnp.broadcast_to((key_ids < suffix_end)[None, :], (dec_count, key_count))
    dec_state = attend_blocks(states[1], dec_queries, key_rows, dec_allow)
    states = (tok_state, dec_state)
    whole_blocks = lax.all_gather(cache, "context", axis=1, tiled=True)
    slot_count = whole_blocks.shape[1]
    cache_key_rows = whole_blocks[0].reshape(slot_count * block_rows, kv_width)
    slot_keep = jnp.repeat(slot_live, block_rows)
    tok_allow = jnp.broadcast_to(slot_keep[None, :], (tok_count, slot_count * block_rows))
    tok_state = attend_blocks(states[0], queries, cache_key_rows, tok_allow)
    dec_allow = jnp.broadcast_to(slot_keep[None, :], (dec_count, slot_count * block_rows))
    dec_state = attend_blocks(states[1], dec_queries, cache_key_rows, dec_allow)
    states = (tok_state, dec_state)
    dec_state = states[1]
    dec_state = attend(dec_state, dec_queries, fresh, dec_ids[None, :] <= dec_ids[:, None])
    return (finish(states[0])[None], finish(dec_state)[None], fresh[None])


def solution(mesh):
    placed = (
        P("pool", "context", None, None),
        P("pool", None),
        P("pool"),
        P("pool"),
        P("pool", "context", None),
        P("pool", "context", "tensor", None),
        P("pool", None, None),
        P(("context", "tensor"), None),
        P(),
        P("pool", None, "tensor", None),
    )
    return jax.shard_map(
        on_device,
        mesh=mesh,
        in_specs=placed,
        out_specs=(
            P("pool", "context", "tensor", None),
            P("pool", None, "tensor", None),
            P("pool", None, None),
        ),
        check_vma=False,
    )
```

profile of v0, /device:TPU:2, one launch (start us, length us, event | category | flops | bytes accessed | tf_op | source)
XLA Modules:
  0.0 293.0 jit_solution(11950341913279943459)
XLA Ops:
  7.3 0.7 all-gather.2.cloned.1.call-update
  8.0 4.1 %copy.91 = bf16[1,64,32,576]{3,1,2,0:T(8,128)(2,1)} copy(bf16[1,64,32,576]{3,2,1,0:T(8,128)(2,1)} %param.21) | data formatting | bytes 4718592 | tf_op args[5]
  13.7 0.9 fusion.42
  14.6 110.2 %psum.7 = f32[2,576]{1,0:T(2,128)S(1)} all-reduce(f32[2,576]{1,0:T(2,128)S(1)} %fusion.42), channel_id=1, replica_groups=mesh['pool'=8,'context'=32,'tensor'=2] {'context','tensor'}, use_global_device_ids=true, to_apply=%region_14.15 | all-reduce | flops 1152 | bytes 9216 | tf_op jit(solution)/shard_map/psum | solution.py:110
  125.1 0.7 pad_maximum_fusion
  125.8 68.4 %all_gather.7 = bf16[1,32,16,576]{3,2,0,1:T(8,128)(2,1)S(1)} all-gather(bf16[1,1,16,576]{3,2,0,1:T(8,128)(2,1)S(1)} %bitcast.129), channel_id=1, replica_groups=mesh['pool'=8,'context'=32,'tensor'=2] {'context'}, dimensions={1}, use_global_device_ids=true | all-gather | bytes 608256 | tf_op jit(solution)/shard_map/all_gather | solution.py:131
  194.5 1.0 fusion.53
  195.5 6.2 %fusion.16 = (f32[64,32]{1,0:T(8,128)}, f32[64,32,512]{2,1,0:T(8,128)}) fusion(pred[512]{0:T(512)(128)(4,1)S(1)} %broadcast_in_dim_reshape.4, bf16[512,576,1]{1,0,2:T(8,128)(2,1)S(1)} %bitcast.124, bf16[1,64,32,576]{3,2,1,0:T(8,128)(2,1)} %param.21), kind=kOutput, calls=%fused_computation.43 | convolution fusion | flops 1211103232 | bytes 7152128 | tf_op jit(solution)/shard_map/rhc,kc->rhk/dot_general | solution.py:16
  201.6 2.9 %copy.69 = bf16[4,512,576]{1,2,0:T(8,128)(2,1)S(1)} copy(bf16[4,512,576]{2,1,0:T(8,128)(2,1)} %bitcast.121) | data formatting | bytes 4718592
  204.6 3.7 %while.30 = (s32[]{:T(128)}, f32[2,32]{1,0:T(2,128)S(1)}, f32[2,32]{1,0:T(2,128)S(1)}, f32[2,32,512]{2,1,0:T(8,128)S(1)}, pred[4,2,512]{2,1,0:T(4,128)(4,1)S(1)}...) while((s32[]{:T(128)}, f32[2,32]{1,0:T(2,128)S(1)}, ...), condition=%wide.region_12.13_spmd.clone, body=%wide.region_9.12_spmd.clone.sunk | while | flops 71762240 | bytes 3043965 | solution.py:43
  208.3 68.3 %conditional.1 = (f32[64,32,512]{2,1,0:T(8,128)}, f32[64,32]{1,0:T(8,128)S(1)}, f32[64,32]{1,0:T(8,128)S(1)}) conditional(s32[]{:T(128)} %convert_element_type.54, () %tuple.24, (bf16[1,2048,576]{2,1,0:T(8,128)(2,1)}, s32[2048]{0:T(1024)S(1)}, s32[]{:T(128)}, s32[64]{0:T(128)S(1)}, bf16[64,32,576]{2,0,1:T(8,128)(2,1)}) %tuple.99), branch_computations={%region_0.0_spmd, %region_1.6_spmd} | conditional | flops 2295474176 | bytes 31089640 | solution.py:127
  208.5 4.3 %copy.58 = bf16[4,512,576]{1,2,0:T(8,128)(2,1)} copy(bf16[4,512,576]{2,1,0:T(8,128)(2,1)} %bitcast.122) | data formatting | bytes 4718592 | tf_op jit(solution)/shard_map/cond
  212.9 63.6 %while.29 = (s32[]{:T(128)}, f32[64,32]{0,1:T(8,128)S(1)}, f32[64,32]{0,1:T(8,128)S(1)}, f32[64,32,512]{2,1,0:T(8,128)}, pred[4,64,512]{2,1,0:T(8,128)(4,1)S(1)}...) while((s32[]{:T(128)}, f32[64,32]{0,1:T(8,128)S(1)}, ...), condition=%wide.region_5.5_spmd.clone, body=%wide.region_2.4_spmd.clone.sunk | while | flops 2295343104 | bytes 26181756 | solution.py:43
  212.9 5.9 %fusion.76 = (f32[64,32]{0,1:T(8,128)S(1)}, f32[512,64,32]{0,1,2:T(8,128)}) fusion(pred[64,512]{1,0:T(8,128)(4,1)S(1)} %dynamic-slice_bitcast_fusion.10, bf16[64,32,576]{2,0,1:T(8,128)(2,1)} %get-tuple-element.394, bf16[4,512,576]{1,2,0:T(8,128)(2,1)} %get-tuple-element.393, s32[]{:T(128)S(6)} %copy.100), kind=kOutput, calls=%fused_computation.5.clone.1 | convolution fusion | flops 1211103232 | bytes 7446532 | tf_op jit(solution)/shard_map/cond/branch_1_fun/while/body/eval_jaxpr/rhc,kc->rhk/dot_general | solution.py:16
  218.8 3.1 %convert_reduce_fusion.8 = (f32[64,32]{0,1:T(8,128)S(1)}, bf16[64,32,512]{2,0,1:T(8,128)(2,1)S(1)}) fusion(f32[64,32]{0,1:T(8,128)S(1)} %select_maximum_fusion.2, f32[512,64,32]{0,1,2:T(8,128)} %get-tuple-element.365, pred[64,512]{1,0:T(8,128)(4,1)S(1)} %dynamic-slice_bitcast_fusion.10), kind=kLoop, calls=%fused_computation.3.clone.1 | loop fusion | flops 7337984 | bytes 6340608 | tf_op jit(solution)/shard_map/cond/branch_1_fun/while/body/eval_jaxpr/reduce_sum | solution.py:24
  222.0 1.1 dynamic-slice_bitcast_fusion.11
  223.1 4.1 %fusion.78 = f32[64,32,512]{2,1,0:T(8,128)} fusion(f32[64,32,512]{2,1,0:T(8,128)} %get-tuple-element.382, bf16[64,32,512]{2,0,1:T(8,128)(2,1)S(1)} %get-tuple-element.368, f32[64,32]{1,0:T(8,128)S(1)} %copy.95, pred[]{:T(512)S(6)} %compare.7, bf16[512,576]{0,1:T(8,128)(2,1)S(1)} %dynamic-slice_bitcast_fusion.11), kind=kOutput, calls=%fused_computation.2.clone.1 | convolution fusion | flops 1076887552 | bytes 11042817 | tf_op jit(solution)/shard_map/cond/branch_1_fun/while/body/eval_jaxpr/rhk,kc->rhc/dot_general | solution.py:25
  227.1 5.9 %fusion.76 = (f32[64,32]{0,1:T(8,128)S(1)}, f32[512,64,32]{0,1,2:T(8,128)}) fusion(pred[64,512]{1,0:T(8,128)(4,1)S(1)} %dynamic-slice_bitcast_fusion.10, bf16[64,32,576]{2,0,1:T(8,128)(2,1)} %get-tuple-element.394, bf16[4,512,576]{1,2,0:T(8,128)(2,1)} %get-tuple-element.393, s32[]{:T(128)S(6)} %copy.100), kind=kOutput, calls=%fused_computation.5.clone.1 | convolution fusion | flops 1211103232 | bytes 7446532 | tf_op jit(solution)/shard_map/cond/branch_1_fun/while/body/eval_jaxpr/rhc,kc->rhk/dot_general | solution.py:16
  233.0 3.1 %convert_reduce_fusion.8 = (f32[64,32]{0,1:T(8,128)S(1)}, bf16[64,32,512]{2,0,1:T(8,128)(2,1)S(1)}) fusion(f32[64,32]{0,1:T(8,128)S(1)} %select_maximum_fusion.2, f32[512,64,32]{0,1,2:T(8,128)} %get-tuple-element.365, pred[64,512]{1,0:T(8,128)(4,1)S(1)} %dynamic-slice_bitcast_fusion.10), kind=kLoop, calls=%fused_computation.3.clone.1 | loop fusion | flops 7337984 | bytes 6340608 | tf_op jit(solution)/shard_map/cond/branch_1_fun/while/body/eval_jaxpr/reduce_sum | solution.py:24
  236.2 1.1 dynamic-slice_bitcast_fusion.11
  237.3 6.3 %fusion.78 = f32[64,32,512]{2,1,0:T(8,128)} fusion(f32[64,32,512]{2,1,0:T(8,128)} %get-tuple-element.382, bf16[64,32,512]{2,0,1:T(8,128)(2,1)S(1)} %get-tuple-element.368, f32[64,32]{1,0:T(8,128)S(1)} %copy.95, pred[]{:T(512)S(6)} %compare.7, bf16[512,576]{0,1:T(8,128)(2,1)S(1)} %dynamic-slice_bitcast_fusion.11), kind=kOutput, calls=%fused_computation.2.clone.1 | convolution fusion | flops 1076887552 | bytes 11042817 | tf_op jit(solution)/shard_map/cond/branch_1_fun/while/body/eval_jaxpr/rhk,kc->rhc/dot_general | solution.py:25
  243.6 5.9 %fusion.76 = (f32[64,32]{0,1:T(8,128)S(1)}, f32[512,64,32]{0,1,2:T(8,128)}) fusion(pred[64,512]{1,0:T(8,128)(4,1)S(1)} %dynamic-slice_bitcast_fusion.10, bf16[64,32,576]{2,0,1:T(8,128)(2,1)} %get-tuple-element.394, bf16[4,512,576]{1,2,0:T(8,128)(2,1)} %get-tuple-element.393, s32[]{:T(128)S(6)} %copy.100), kind=kOutput, calls=%fused_computation.5.clone.1 | convolution fusion | flops 1211103232 | bytes 7446532 | tf_op jit(solution)/shard_map/cond/branch_1_fun/while/body/eval_jaxpr/rhc,kc->rhk/dot_general | solution.py:16
  249.4 3.1 %convert_reduce_fusion.8 = (f32[64,32]{0,1:T(8,128)S(1)}, bf16[64,32,512]{2,0,1:T(8,128)(2,1)S(1)}) fusion(f32[64,32]{0,1:T(8,128)S(1)} %select_maximum_fusion.2, f32[512,64,32]{0,1,2:T(8,128)} %get-tuple-element.365, pred[64,512]{1,0:T(8,128)(4,1)S(1)} %dynamic-slice_bitcast_fusion.10), kind=kLoop, calls=%fused_computation.3.clone.1 | loop fusion | flops 7337984 | bytes 6340608 | tf_op jit(solution)/shard_map/cond/branch_1_fun/while/body/eval_jaxpr/reduce_sum | solution.py:24
  252.6 1.1 dynamic-slice_bitcast_fusion.11
  253.7 6.3 %fusion.78 = f32[64,32,512]{2,1,0:T(8,128)} fusion(f32[64,32,512]{2,1,0:T(8,128)} %get-tuple-element.382, bf16[64,32,512]{2,0,1:T(8,128)(2,1)S(1)} %get-tuple-element.368, f32[64,32]{1,0:T(8,128)S(1)} %copy.95, pred[]{:T(512)S(6)} %compare.7, bf16[512,576]{0,1:T(8,128)(2,1)S(1)} %dynamic-slice_bitcast_fusion.11), kind=kOutput, calls=%fused_computation.2.clone.1 | convolution fusion | flops 1076887552 | bytes 11042817 | tf_op jit(solution)/shard_map/cond/branch_1_fun/while/body/eval_jaxpr/rhk,kc->rhc/dot_general | solution.py:25
  260.0 5.9 %fusion.76 = (f32[64,32]{0,1:T(8,128)S(1)}, f32[512,64,32]{0,1,2:T(8,128)}) fusion(pred[64,512]{1,0:T(8,128)(4,1)S(1)} %dynamic-slice_bitcast_fusion.10, bf16[64,32,576]{2,0,1:T(8,128)(2,1)} %get-tuple-element.394, bf16[4,512,576]{1,2,0:T(8,128)(2,1)} %get-tuple-element.393, s32[]{:T(128)S(6)} %copy.100), kind=kOutput, calls=%fused_computation.5.clone.1 | convolution fusion | flops 1211103232 | bytes 7446532 | tf_op jit(solution)/shard_map/cond/branch_1_fun/while/body/eval_jaxpr/rhc,kc->rhk/dot_general | solution.py:16
  265.9 3.1 %convert_reduce_fusion.8 = (f32[64,32]{0,1:T(8,128)S(1)}, bf16[64,32,512]{2,0,1:T(8,128)(2,1)S(1)}) fusion(f32[64,32]{0,1:T(8,128)S(1)} %select_maximum_fusion.2, f32[512,64,32]{0,1,2:T(8,128)} %get-tuple-element.365, pred[64,512]{1,0:T(8,128)(4,1)S(1)} %dynamic-slice_bitcast_fusion.10), kind=kLoop, calls=%fused_computation.3.clone.1 | loop fusion | flops 7337984 | bytes 6340608 | tf_op jit(solution)/shard_map/cond/branch_1_fun/while/body/eval_jaxpr/reduce_sum | solution.py:24
  269.1 1.1 dynamic-slice_bitcast_fusion.11
  270.2 6.3 %fusion.78 = f32[64,32,512]{2,1,0:T(8,128)} fusion(f32[64,32,512]{2,1,0:T(8,128)} %get-tuple-element.382, bf16[64,32,512]{2,0,1:T(8,128)(2,1)S(1)} %get-tuple-element.368, f32[64,32]{1,0:T(8,128)S(1)} %copy.95, pred[]{:T(512)S(6)} %compare.7, bf16[512,576]{0,1:T(8,128)(2,1)S(1)} %dynamic-slice_bitcast_fusion.11), kind=kOutput, calls=%fused_computation.2.clone.1 | convolution fusion | flops 1076887552 | bytes 11042817 | tf_op jit(solution)/shard_map/cond/branch_1_fun/while/body/eval_jaxpr/rhk,kc->rhc/dot_general | solution.py:25
  276.7 3.5 %convert_reduce_fusion.2 = f32[64,32]{1,0:T(8,128)S(1)} fusion(f32[64,32]{1,0:T(8,128)S(1)} %max.15, f32[64,32,512]{2,1,0:T(8,128)} %get-tuple-element.259, pred[512]{0:T(512)(128)(4,1)S(1)} %broadcast_in_dim_reshape.4), kind=kLoop, calls=%fused_computation.40 | loop fusion | flops 7337984 | bytes 4211200 | tf_op jit(solution)/shard_map/reduce_sum | solution.py:24
  280.5 4.5 %fusion.19 = bf16[1,64,32,512]{3,2,1,0:T(8,128)(2,1)} fusion(f32[64,32]{1,0:T(8,128)S(1)} %get-tuple-element.250, f32[64,32,512]{2,1,0:T(8,128)} %get-tuple-element.101, f32[64,32]{1,0:T(8,128)S(1)} %get-tuple-element.251, bf16[512,576]{1,0:T(8,128)(2,1)S(1)} %bitcast.125, f32[64,32,512]{2,1,0:T(8,128)S(1)} %copy-done.1, f32[64,32]{1,0:T(8,128)S(1)} %max.15, ...), kind=kOutput, calls=%fused_computation.47 | convolution fusion | flops 1083179008 | bytes 11108864 | tf_op jit(solution)/shard_map/rhk,kc->rhc/dot_general | solution.py:25
  285.3 0.8 fusion.24
  (105 shorter events, 5.8 us)
Async XLA Ops:
  7.2 6.5 %copy-start = (bf16[112,576]{1,0:T(8,128)(2,1)S(1)}, bf16[112,576]{1,0:T(8,128)(2,1)}, u32[]{:S(2)}) copy-start(bf16[112,576]{1,0:T(8,128)(2,1)} %param.23) | copy-start | bytes 387076
  7.2 5.6 %copy-start.7 = (s32[1,32]{1,0:T(1,128)S(1)}, s32[1,32]{1,0:T(1,128)}, u32[]{:S(2)}) copy-start(s32[1,32]{1,0:T(1,128)} %param.17) | copy-start | bytes 388
  7.2 117.9 %copy-start.6 = (f32[512]{0:T(512)S(1)}, f32[512]{0:T(512)}, u32[]{:S(2)}) copy-start(f32[512]{0:T(512)} %param.24) | copy-start | bytes 6148
  7.2 118.6 %copy-start.5 = (bf16[1,1,16,576]{3,2,1,0:T(8,128)(2,1)S(1)}, bf16[1,1,16,576]{3,2,1,0:T(8,128)(2,1)}, u32[]{:S(2)}) copy-start(bf16[1,1,16,576]{3,2,1,0:T(8,128)(2,1)} %param.16) | copy-start | bytes 55300
  7.2 187.1 %copy-start.2 = (bf16[1,2,32,576]{3,2,1,0:T(8,128)(2,1)S(1)}, bf16[1,2,32,576]{3,2,1,0:T(8,128)(2,1)}, u32[]{:S(2)}) copy-start(bf16[1,2,32,576]{3,2,1,0:T(8,128)(2,1)} %param.25) | copy-start | bytes 221188
  7.2 194.4 %all-gather.2.cloned.1.call-start = ((), (), s32[]{:S(2)}) async-start(), calls=%async_computation | async-start | bytes 2703360 | tf_op jit(solution)/shard_map/all_gather | solution.py:116
  208.3 68.3 %copy-start.4 = (f32[64,32]{1,0:T(8,128)S(1)}, f32[64,32]{1,0:T(8,128)}, u32[]{:S(2)}) copy-start(f32[64,32]{1,0:T(8,128)} %get-tuple-element.258) | copy-start | bytes 24580
  276.6 3.7 %copy-start.3 = (f32[2,32,512]{2,1,0:T(8,128)S(1)}, f32[2,32,512]{2,1,0:T(8,128)}, u32[]{:S(2)}) copy-start(f32[2,32,512]{2,1,0:T(8,128)} %get-tuple-element.263) | copy-start | bytes 393220
  276.6 3.9 %copy-start.1 = (f32[64,32,512]{2,1,0:T(8,128)S(1)}, f32[64,32,512]{2,1,0:T(8,128)}, u32[]{:S(2)}) copy-start(f32[64,32,512]{2,1,0:T(8,128)} %get-tuple-element.259) | copy-start | bytes 12582916
Sparse Core Ops, SparseCore 0:
  11.2 87.6 all-gather.1
where the time goes:
time: 294 us; the launch traced here: 293 us
  blocking collectives  179 us (61%)
  matrix products  62.6 us (21%)
  other arithmetic  18.3 us (6%)
  local copies, waits for them, and re-layouts  16.8 us (6%)
  between operations  15.6 us (5%)
    psum x1, blocking collectives, on_device(): lax.psum(jnp.dot(hidden_part, kv_down, preferred_element_type=jnp.float32...  110 us
    all_gather x1, blocking collectives, on_device(): whole_blocks = lax.all_gather(cache, 'context', axis=1, tiled=True)  68.4 us
    dot_general x11, matrix products, attend(): jnp.einsum('rhc,kc->rhk', queries, key_rows, preferred_element_type=jnp.f...  32.1 us
    dot_general x11, matrix products, attend(): jnp.einsum('rhk,kc->rhc', weights, key_rows[:, :lat_width], preferred_ele...  29.6 us
    reduce_sum x11, other arithmetic, attend(): jnp.sum(weights.astype(jnp.float32), axis=-1)  16.8 us
    unnamed x18, local copies, waits for them, and re-layouts  7.07 us
  transfers between devices with their start and end apart: 1, of which 0 were waited for; matrix products, arithmetic and copies ran while one was open for 5% of the time, Pallas kernels for 0%

commit v1 on v0

v1 whole, which is shorter than its diff:
```python
import functools

import jax
import jax.numpy as jnp
from jax import lax
from jax.experimental import pallas as pl
from jax.experimental.pallas import tpu as pltpu
from jax.sharding import PartitionSpec as P

SCALE2 = 192.0 ** (-0.5) * 1.4426950408889634
BIG = -1e38
MESH = pl.DeviceIdType.MESH

NX, NY = 4, 8
TOK, HEADS, KVW, LAT, WIDE = 64, 32, 576, 512, 640
ROWS = TOK * HEADS
DROWS = 2 * HEADS
A_ROWS, B_ROWS = 48, 32
A_GROUP, B_GROUP = NY * A_ROWS, NX * B_ROWS
B_BASE = NX * A_GROUP
KEYS = B_BASE + NY * B_GROUP
QBLK = 512
KSUB = 256


A_STEP = ((0, 48), (48, 96), (144, 96), (240, 96), (336, 48))
B_SUB = ((0, 32), (32, 64), (96, 32))


def a_off(group, row):
    return group * A_GROUP + row


def b_off(group, row):
    return B_BASE + group * B_GROUP + row


def minus(step):
    return 2 * step - 1 if step else 0


def plus(step):
    return 2 * step


def message_plan():
    plan = {}
    for s in (1, 2, 3):
        plan["ayM", s] = (a_off(0, minus(s - 1) * 48), a_off(0, minus(s) * 48), 48, "y+")
        plan["ayP", s] = (a_off(0, plus(s - 1) * 48), a_off(0, plus(s) * 48), 48, "y-")
    plan["ayM", 4] = (a_off(0, minus(3) * 48), a_off(0, 336), 32, "y+")
    plan["ayP", 4] = (a_off(0, plus(3) * 48 + 32), a_off(0, 368), 16, "y-")
    far = (((0, 32), (32, 16)), ((48, 48), (96, 48)), ((144, 48), (192, 48)), ((240, 48), (288, 48)), ((336, 16), (352, 32)))
    for s in range(5):
        row, count = A_STEP[s]
        plan["axM", s] = (a_off(0, row), a_off(1, row), count, "x+")
        plan["axP", s] = (a_off(0, row), a_off(2, row), count, "x-")
        (row_m, count_m), (row_p, count_p) = far[s]
        plan["axxM", s] = (a_off(1, row_m), a_off(3, row_m), count_m, "x+")
        plan["axxP", s] = (a_off(2, row_p), a_off(3, row_p), count_p, "x-")
        for g in range(4):
            if (g, s) != (0, 0):
                plan["as", g, s] = (a_off(g, row), a_off(g, row), count, "core")
    plan["bxM", 1] = (b_off(0, 0), b_off(0, 32), 32, "x+")
    plan["bxP", 1] = (b_off(0, 0), b_off(0, 64), 32, "x-")
    plan["bxM", 2] = (b_off(0, 32), b_off(0, 96), 16, "x+")
    plan["bxP", 2] = (b_off(0, 64 + 16), b_off(0, 96 + 16), 16, "x-")
    halves = (((0, 16), (16, 16)), ((32, 32), (64, 32)), ((96, 16), (112, 16)))
    for u in range(3):
        row, count = B_SUB[u]
        for s in (1, 2, 3):
            plan["byM", s, u] = (b_off(minus(s - 1), row), b_off(minus(s), row), count, "y+")
            plan["byP", s, u] = (b_off(plus(s - 1), row), b_off(plus(s), row), count, "y-")
        (row_m, count_m), (row_p, count_p) = halves[u]
        plan["byM", 4, u] = (b_off(minus(3), row_m), b_off(7, row_m), count_m, "y+")
        plan["byP", 4, u] = (b_off(plus(3), row_p), b_off(7, row_p), count_p, "y-")
        for g in range(8):
            if (g, u) != (0, 0):
                plan["bs", g, u] = (b_off(g, row), b_off(g, row), count, "core")
    return plan


PLAN = message_plan()
INDEX = {name: i for i, name in enumerate(PLAN)}


def events_a():
    out = [("send", ("ayM", 1)), ("send", ("ayP", 1)), ("send", ("axM", 0)), ("send", ("axP", 0)), ("sum",)]

    def near(s):
        out.extend([("wait", ("axM", s)), ("send", ("axxM", s)), ("send", ("as", 1, s))])
        out.extend([("wait", ("axP", s)), ("send", ("axxP", s)), ("send", ("as", 2, s))])

    def far(s):
        out.extend([("wait", ("axxM", s)), ("wait", ("axxP", s)), ("send", ("as", 3, s))])

    for s in (1, 2, 3, 4):
        out.append(("wait", ("ayM", s)))
        if s < 4:
            out.append(("send", ("ayM", s + 1)))
        out.append(("wait", ("ayP", s)))
        if s < 4:
            out.append(("send", ("ayP", s + 1)))
        out.extend([("send", ("axM", s)), ("send", ("axP", s)), ("send", ("as", 0, s))])
        near(s - 1)
        if s >= 2:
            far(s - 2)
        out.append(("sum",))
    near(4)
    out.append(("sum",))
    far(3)
    far(4)
    return out


def events_b():
    out = [("send", ("bxM", 1)), ("send", ("bxP", 1)), ("send", ("byM", 1, 0)), ("send", ("byP", 1, 0)), ("sum",)]
    out.extend([("wait", ("bxM", 1)), ("send", ("bxM", 2)), ("wait", ("bxP", 1)), ("send", ("bxP", 2))])
    out.extend([("send", ("byM", 1, 1)), ("send", ("byP", 1, 1)), ("send", ("bs", 0, 1))])

    def hop(s, u):
        out.append(("wait", ("byM", s, u)))
        if s < 4:
            out.extend([("send", ("byM", s + 1, u)), ("send", ("bs", minus(s), u))])
        out.append(("wait", ("byP", s, u)))
        if s < 4:
            out.extend([("send", ("byP", s + 1, u)), ("send", ("bs", plus(s), u))])
        else:
            out.append(("send", ("bs", 7, u)))

    hop(1, 0)
    out.append(("sum",))
    out.extend([("wait", ("bxM", 2)), ("wait", ("bxP", 2))])
    out.extend([("send", ("byM", 1, 2)), ("send", ("byP", 1, 2)), ("send", ("bs", 0, 2))])
    for diagonal in range(2, 7):
        for u in (2, 1, 0):
            if 1 <= diagonal - u <= 4:
                hop(diagonal - u, u)
        if diagonal < 6:
            out.append(("sum",))
    return out


def gather_kernel(
    hits_ref,
    prefix_ref,
    slen_ref,
    suffix_ref,
    cache_ref,
    hidden_ref,
    down_ref,
    dq_ref,
    q_ref,
    key_ref,
    qa_ref,
    raw_ref,
    q_in,
    part_send,
    part_recv,
    send_sem,
    recv_sem,
    psend_sem,
    precv_sem,
    q_sem,
):
    pool = lax.axis_index("pool")
    ctx = lax.axis_index("context")
    core = lax.axis_index("tensor")
    x, y = ctx // NY, ctx % NY
    x_plus, x_minus = (x + 1) % NX, (x + NX - 1) % NX
    y_plus, y_minus = (y + 1) % NY, (y + NY - 1) % NY
    place = {
        "x+": (pool, x_plus * NY + y, core),
        "x-": (pool, x_minus * NY + y, core),
        "y+": (pool, x * NY + y_plus, core),
        "y-": (pool, x * NY + y_minus, core),
        "core": (pool, ctx, 1 - core),
    }
    x_pair = x + 1 - 2 * (x % 2)
    y_pair = y + 1 - 2 * (y % 2)
    y_four = (y // 4) * 4 + 3 - y % 4
    fold = [
        place["core"],
        (pool, x_pair * NY + y, core),
        (pool, (NX - 1 - x) * NY + y, core),
        (pool, x * NY + y_pair, core),
        (pool, x * NY + y_four, core),
        (pool, x * NY + NY - 1 - y, core),
    ]

    q_copy = pltpu.make_async_copy(q_ref, q_in, q_sem)
    q_copy.start()

    barrier = pltpu.get_barrier_semaphore()
    friends = list(place.values()) + fold[4:]
    for friend in friends:
        pl.semaphore_signal(barrier, inc=1, device_id=friend, device_id_type=MESH)

    prefix = prefix_ref[0]
    slen = slen_ref[0]
    lane = lax.broadcasted_iota(jnp.int32, (TOK, TOK), 1)
    token = lax.broadcasted_iota(jnp.int32, (TOK, TOK), 0) + ctx * TOK
    hidden_here = ((lane < 32) & (ctx > lane)) | ((lane == 32) & (token >= slen))
    tail = jnp.where(hidden_here, BIG, 0.0).astype(jnp.bfloat16)
    own = jnp.concatenate([suffix_ref[...], tail], axis=1)
    order = lax.broadcasted_iota(jnp.int32, (1, 32), 1)
    hit = jnp.where((hits_ref[...] == ctx) & (order < prefix), 1.0, 0.0)
    live = jnp.max(hit, axis=1, keepdims=True)
    dead = jnp.broadcast_to(jnp.where(live > 0.5, 0.0, BIG), (16, TOK)).astype(jnp.bfloat16)
    own_cache = jnp.concatenate([cache_ref[...], dead], axis=1)
    key_ref[0:32, :] = own[0:32]
    key_ref[32:48, :] = own_cache
    key_ref[B_BASE : B_BASE + 32, :] = own[32:64]

    part = ctx * 2 + core
    lane_block = jnp.minimum((part * 112) // 128, 54)
    shift = part * 112 - lane_block * 128
    window = hidden_ref[:, pl.ds(pl.multiple_of(lane_block * 128, 128), 256)]
    pick = lax.broadcasted_iota(jnp.int32, (256, 112), 0) == lax.broadcasted_iota(jnp.int32, (256, 112), 1) + shift
    pick = jnp.where(pick, 1.0, 0.0).astype(jnp.bfloat16)
    piece = jnp.dot(window, pick, preferred_element_type=jnp.float32).astype(jnp.bfloat16)
    partial = jnp.dot(piece, down_ref[...], preferred_element_type=jnp.float32)
    part_send[...] = jnp.zeros_like(part_send)
    part_send[0, 0:2, 0:KVW] = partial

    pl.semaphore_wait(barrier, len(friends))

    def copy_of(name):
        source, target, count, where = PLAN[name]
        i = INDEX[name]
        return pltpu.make_async_remote_copy(
            src_ref=key_ref.at[pl.ds(source, count)],
            dst_ref=key_ref.at[pl.ds(target, count)],
            send_sem=send_sem.at[i],
            recv_sem=recv_sem.at[i],
            device_id=place[where],
            device_id_type=MESH,
        )

    def fold_copy(i):
        return pltpu.make_async_remote_copy(
            src_ref=part_send.at[i],
            dst_ref=part_recv.at[i],
            send_sem=psend_sem.at[i],
            recv_sem=precv_sem.at[i],
            device_id=fold[i],
            device_id_type=MESH,
        )

    def fold_step(i):
        if i > 0:
            fold_copy(i - 1).wait_recv()
            total = part_send[i - 1] + part_recv[i - 1]
            if i < 6:
                part_send[i] = total
            else:
                raw_ref[...] = total
        if i < 6:
            fold_copy(i).start()

    def run(events):
        sums = 0
        for event in events:
            if event[0] == "send":
                copy_of(event[1]).start()
            elif event[0] == "wait":
                copy_of(event[1]).wait_recv()
            else:
                fold_step(sums)
                sums += 1
        return sums

    def sends(events):
        return [event[1] for event in events if event[0] == "send"]

    plan_a, plan_b = events_a(), events_b()

    def side(mine, other):
        done = run(mine)
        q_copy.wait()
        lanes = lax.broadcasted_iota(jnp.int32, (256, TOK), 1)
        pick_rank = jnp.where(lanes == ctx, 1.0, 0.0).astype(jnp.bfloat16)

        def widen(i, carry):
            rows = pl.ds(pl.multiple_of(i * 256, 256), 256)
            qa_ref[rows, :] = jnp.concatenate([q_in[rows, :], pick_rank], axis=1)
            return carry

        lax.fori_loop(0, ROWS // 256, widen, 0)
        pick_dec = jnp.where(lanes[0:DROWS] == 32, 1.0, 0.0).astype(jnp.bfloat16)
        qa_ref[ROWS : ROWS + DROWS, :] = jnp.concatenate([dq_ref[...], pick_dec], axis=1)
        for i in range(done, 7):
            fold_step(i)
        for name in sends(other):
            if PLAN[name][3] == "core":
                copy_of(name).wait_recv()
        for name in sends(mine):
            copy_of(name).wait_send()
        for i in range(6):
            fold_copy(i).wait_send()

    @pl.when(core == 0)
    def _():
        side(plan_a, plan_b)

    @pl.when(core == 1)
    def _():
        side(plan_b, plan_a)


def attend_kernel(
    prefix_ref, slen_ref, key_ref, qa_ref, raw_ref, gain_ref, out_ref, dec_ref, fresh_ref, s0, s1, p0, p1, m_ref, l_ref, o_ref, out_sem
):
    blocks = ROWS // QBLK
    first = [b * QBLK for b in range(blocks)]
    count = [QBLK] * (blocks - 1) + [QBLK + DROWS]
    score, weight = [s0, s1], [p0, p1]
    dims = (((1,), (1,)), ((), ()))
    subs = KEYS // KSUB

    def scores(b, j):
        n = count[b]
        s = lax.dot_general(
            qa_ref[first[b] : first[b] + n, :], key_ref[j * KSUB : (j + 1) * KSUB, :], dims, preferred_element_type=jnp.float32
        )
        base = 0 if j == 0 else (32 if j * KSUB == B_BASE else None)
        if base is not None:
            row = lax.broadcasted_iota(jnp.int32, (n, 128), 0)
            col = lax.broadcasted_iota(jnp.int32, (n, 128), 1)
            tok = (row + first[b]) // HEADS
            mask = (col < 32) & (col + base > tok) & (tok < TOK)
            head = jnp.where(mask, BIG, s[:, 0:128])
            score[b % 2][0:n, j * KSUB : j * KSUB + 128] = head
            score[b % 2][0:n, j * KSUB + 128 : (j + 1) * KSUB] = s[:, 128:]
        else:
            score[b % 2][0:n, j * KSUB : (j + 1) * KSUB] = s

    def row_max(b):
        n = count[b]
        m_ref[b % 2, 0:n] = jnp.max(score[b % 2][0:n, :], axis=1, keepdims=True) * SCALE2

    def soft(b, j, total):
        n = count[b]
        s = score[b % 2][0:n, j * KSUB : (j + 1) * KSUB]
        p = jnp.exp2(s * SCALE2 - m_ref[b % 2, 0:n])
        weight[b % 2][0:n, j * KSUB : (j + 1) * KSUB] = p.astype(jnp.bfloat16)
        return total + jnp.sum(p, axis=1, keepdims=True)

    def fresh_rows():
        raw = raw_ref[...]
        latent = raw[:, 0:LAT]
        norm = latent * lax.rsqrt(jnp.sum(latent * latent, axis=1, keepdims=True) * (1.0 / LAT) + 1e-06) * gain_ref[...]
        tail = raw[:, LAT:WIDE]
        lane = lax.broadcasted_iota(jnp.int32, (8, 128), 1)
        step = lax.broadcasted_iota(jnp.int32, (8, 128), 0)
        pos = (prefix_ref[0] * 16 + slen_ref[0] + step).astype(jnp.float32)
        freq = jnp.exp((lane % 32).astype(jnp.float32) * (-9.210340371976184 / 32.0))
        angle = pos * freq
        cosine, sine = jnp.cos(angle), jnp.sin(angle)
        ahead = pltpu.roll(tail, 96, 1)
        behind = pltpu.roll(tail, 32, 1)
        turned = jnp.where(lane < 32, tail * cosine - ahead * sine, tail * cosine + behind * sine)
        turned = jnp.where(lane < 64, turned, 0.0)
        return jnp.concatenate([norm, turned], axis=1).astype(jnp.bfloat16)

    def context(b):
        n = count[b]
        acc = jnp.dot(weight[b % 2][0:n, :], key_ref[:, 0:LAT], preferred_element_type=jnp.float32)
        total = l_ref[b % 2, 0:n]
        o_ref[first[b] : first[b] + QBLK, :] = (acc[0:QBLK] / total[0:QBLK]).astype(jnp.bfloat16)
        out_copy(b).start()
        if n > QBLK:
            fresh = fresh_rows()
            fresh_ref[...] = fresh[0:2, 0:KVW]
            sf = lax.dot_general(qa_ref[ROWS : ROWS + DROWS, :], fresh, dims, preferred_element_type=jnp.float32) * SCALE2
            row = lax.broadcasted_iota(jnp.int32, (DROWS, 8), 0) // HEADS
            col = lax.broadcasted_iota(jnp.int32, (DROWS, 8), 1)
            sf = jnp.where(col <= row, sf, BIG)
            old = m_ref[b % 2, QBLK:n]
            new = jnp.maximum(old, jnp.max(sf, axis=1, keepdims=True))
            pf = jnp.exp2(sf - new)
            fade = jnp.exp2(old - new)
            total_dec = total[QBLK:n] * fade + jnp.sum(pf, axis=1, keepdims=True)
            more = jnp.dot(pf.astype(jnp.bfloat16), fresh[:, 0:LAT], preferred_element_type=jnp.float32)
            dec_ref[...] = ((acc[QBLK:n] * fade + more) / total_dec).astype(jnp.bfloat16)

    def out_copy(b):
        rows = pl.ds(first[b], QBLK)
        return pltpu.make_async_copy(o_ref.at[rows], out_ref.at[rows], out_sem.at[b])

    for t in range(blocks + 1):
        total = 0.0
        for j in range(subs):
            if t < blocks:
                scores(t, j)
            if t >= 1:
                total = soft(t - 1, j, total)
        if t >= 1:
            l_ref[(t - 1) % 2, 0 : count[t - 1]] = total
            context(t - 1)
        if t < blocks:
            row_max(t)
    for b in range(blocks):
        out_copy(b).wait()


def on_device(
    cache,
    hit_slots,
    prefix_blocks,
    suffix_len,
    suffix_latent,
    suffix_query,
    decode_hidden,
    kv_down,
    kv_gain,
    decode_query,
):
    vmem = pl.BlockSpec(memory_space=pltpu.VMEM)
    smem = pl.BlockSpec(memory_space=pltpu.SMEM)
    anywhere = pl.BlockSpec(memory_space=pl.ANY)
    bf16, f32 = jnp.bfloat16, jnp.float32
    messages = len(PLAN)
    keys, queries, raw = pl.pallas_call(
        gather_kernel,
        name="gather_keys",
        in_specs=[vmem, smem, smem, vmem, vmem, vmem, vmem, vmem, anywhere],
        out_specs=[vmem, vmem, vmem],
        out_shape=[
            pltpu.VMEM((KEYS, WIDE), bf16),
            pltpu.VMEM((ROWS + DROWS, WIDE), bf16),
            pltpu.VMEM((8, WIDE), f32),
        ],
        scratch_shapes=[
            pltpu.VMEM((ROWS, KVW), bf16),
            pltpu.VMEM((6, 8, WIDE), f32),
            pltpu.VMEM((6, 8, WIDE), f32),
            pltpu.SemaphoreType.DMA((messages,)),
            pltpu.SemaphoreType.DMA((messages,)),
            pltpu.SemaphoreType.DMA((6,)),
            pltpu.SemaphoreType.DMA((6,)),
            pltpu.SemaphoreType.DMA,
        ],
        compiler_params=pltpu.CompilerParams(
            collective_id=0, has_side_effects=True, vmem_limit_bytes=24 * 2**20
        ),
    )(
        hit_slots,
        prefix_blocks,
        suffix_len,
        suffix_latent[0],
        cache[0, 0],
        decode_hidden[0],
        kv_down,
        decode_query.reshape(DROWS, KVW),
        suffix_query.reshape(ROWS, KVW),
    )
    tall = QBLK + DROWS
    out, dec, fresh = pl.pallas_call(
        attend_kernel,
        name="attend",
        in_specs=[smem, smem, vmem, vmem, vmem, vmem],
        out_specs=[anywhere, vmem, vmem],
        out_shape=[
            jax.ShapeDtypeStruct((ROWS, LAT), bf16),
            jax.ShapeDtypeStruct((DROWS, LAT), bf16),
            jax.ShapeDtypeStruct((2, KVW), bf16),
        ],
        scratch_shapes=[pltpu.VMEM((tall, KEYS), f32)] * 2
        + [pltpu.VMEM((tall, KEYS), bf16)] * 2
        + [pltpu.VMEM((2, tall, 1), f32)] * 2
        + [pltpu.VMEM((ROWS, LAT), bf16), pltpu.SemaphoreType.DMA((ROWS // QBLK,))],
        compiler_params=pltpu.CompilerParams(vmem_limit_bytes=44 * 2**20),
    )(prefix_blocks, suffix_len, keys, queries, raw, kv_gain.reshape(1, LAT))
    return (
        out.reshape(1, TOK, HEADS, LAT),
        dec.reshape(1, 2, HEADS, LAT),
        fresh.reshape(1, 2, KVW),
    )


def solution(mesh):
    placed = (
        P("pool", "context", None, None),
        P("pool", None),
        P("pool"),
        P("pool"),
        P("pool", "context", None),
        P("pool", "context", "tensor", None),
        P("pool", None, None),
        P(("context", "tensor"), None),
        P(),
        P("pool", None, "tensor", None),
    )
    return jax.shard_map(
        on_device,
        mesh=mesh,
        in_specs=placed,
        out_specs=(
            P("pool", "context", "tensor", None),
            P("pool", None, "tensor", None),
            P("pool", None, None),
        ),
        check_vma=False,
    )
```

time: 294 us -> 59.3 us (0.20)
  blocking collectives: 179 us -> 0 us
  matrix products: 62.6 us -> 0 us
  Pallas kernels: 0 us -> 50.3 us
  other arithmetic: 18.3 us -> 0 us
  between operations: 15.6 us -> 1.98 us
  local copies, waits for them, and re-layouts: 16.8 us -> 6.55 us
    psum x1 -> x0, blocking collectives: 110 us -> none  [on_device(): lax.psum(jnp.dot(hidden_part, kv_down, preferred_element_type=jnp.float32...]
    all_gather x1 -> x0, blocking collectives: 68.4 us -> none  [on_device(): whole_blocks = lax.all_gather(cache, 'context', axis=1, tiled=True)]
    dot_general x23 -> x0, matrix products: 62.6 us -> none  [the longest x11 32.1 us: attend(): jnp.einsum('rhc,kc->rhk', queries, key_rows, preferred_element_type=jnp.f...]
    pallas_call x0 -> x2, Pallas kernels: none -> 50.3 us  [the longest x1 33.5 us: on_device(): pl.pallas_call(gather_kernel, name='gather_keys', in_specs=[vmem, smem, s...]
    reduce_sum x12 -> x0, other arithmetic: 16.9 us -> none  [the longest x11 16.8 us: attend(): jnp.sum(weights.astype(jnp.float32), axis=-1)]
    squeeze x8 -> x0, local copies, waits for them, and re-layouts: 4.62 us -> none  [attend_blocks(): state, unused = lax.scan(advance, state, (key_blocks, allow_blocks))]
    cond x3 -> x0, local copies, waits for them, and re-layouts: 4.5 us -> none
    unnamed x18 -> x16, local copies, waits for them, and re-layouts: 7.07 us -> 6.55 us
  transfers between devices with their start and end apart: 1 -> 0, of which waited for: 0 -> 0; matrix products, arithmetic and copies ran while one was open for 5% -> 0% of each run, Pallas kernels for 0% -> 0%
where the time goes in v1:
time: 59.3 us; the launch traced here: 58.9 us
  Pallas kernels  50.3 us (85%)
  local copies, waits for them, and re-layouts  6.55 us (11%)
  between operations  1.98 us (3%)
    pallas_call x1, Pallas kernels, on_device(): pl.pallas_call(gather_kernel, name='gather_keys', in_specs=[vmem, smem, s...  33.5 us
    pallas_call x1, Pallas kernels, on_device(): pl.pallas_call(attend_kernel, name='attend', in_specs=[smem, smem, vmem,...  16.9 us
    unnamed x16, local copies, waits for them, and re-layouts  6.55 us

profile of v1, /device:TPU:2, one launch (start us, length us, event | category | flops | bytes accessed | tf_op | source)
XLA Modules:
  0.0 58.9 jit_solution(10653862336401425339)
XLA Ops:
  0.6 0.0 copy-start.6
  1.9 0.0 copy-start
  2.0 1.7 %copy-done = bf16[1,64,32,576]{3,2,1,0:T(8,128)(2,1)S(1)} copy-done((bf16[1,64,32,576]{3,2,1,0:T(8,128)(2,1)S(1)}, bf16[1,64,32,576]{3,2,1,0:T(8,128)(2,1)}, u32[]{:S(2)}) %copy-start) | copy-done | bytes 2359320
  3.7 0.0 copy-start.1
  3.7 0.9 %copy-done.1 = bf16[112,576]{1,0:T(8,128)(2,1)S(1)} copy-done((bf16[112,576]{1,0:T(8,128)(2,1)S(1)}, bf16[112,576]{1,0:T(8,128)(2,1)}, u32[]{:S(2)}) %copy-start.1) | copy-done | bytes 129048
  4.6 0.0 copy-start.2
  4.6 0.9 %copy-done.2 = bf16[1,64,576]{2,1,0:T(8,128)(2,1)S(1)} copy-done((bf16[1,64,576]{2,1,0:T(8,128)(2,1)S(1)}, bf16[1,64,576]{2,1,0:T(8,128)(2,1)}, u32[]{:S(2)}) %copy-start.2) | copy-done | bytes 73752
  5.5 0.0 copy-start.3
  5.5 0.9 %copy-done.3 = bf16[1,2,32,576]{3,2,1,0:T(8,128)(2,1)S(1)} copy-done((bf16[1,2,32,576]{3,2,1,0:T(8,128)(2,1)S(1)}, bf16[1,2,32,576]{3,2,1,0:T(8,128)(2,1)}, u32[]{:S(2)}) %copy-start.3) | copy-done | bytes 73752
  6.4 0.0 copy-start.4
  6.4 0.7 %copy-done.4 = bf16[1,2,7168]{2,1,0:T(2,128)(2,1)S(1)} copy-done((bf16[1,2,7168]{2,1,0:T(2,128)(2,1)S(1)}, bf16[1,2,7168]{2,1,0:T(2,128)(2,1)}, u32[]{:S(2)}) %copy-start.4) | copy-done | bytes 28696
  7.1 0.0 copy-start.5
  7.1 0.7 %copy-done.5 = bf16[1,1,16,576]{3,2,1,0:T(8,128)(2,1)S(1)} copy-done((bf16[1,1,16,576]{3,2,1,0:T(8,128)(2,1)S(1)}, bf16[1,1,16,576]{3,2,1,0:T(8,128)(2,1)}, u32[]{:S(2)}) %copy-start.5) | copy-done | bytes 18456
  7.8 0.0 copy-start.7
  7.9 0.7 %copy-done.7 = s32[1,32]{1,0:T(1,128)S(1)} copy-done((s32[1,32]{1,0:T(1,128)S(1)}, s32[1,32]{1,0:T(1,128)}, u32[]{:S(2)}) %copy-start.7) | copy-done | bytes 152
  8.5 33.5 %gather_keys.1 = (bf16[2560,640]{1,0:T(8,128)(2,1)S(1)}, bf16[2112,640]{1,0:T(8,128)(2,1)S(1)}, f32[8,640]{1,0:T(8,128)S(1)}) custom-call(s32[1,32]{1,0:T(1,128)S(1)} %copy-done.7, s32[1]{0:T(128)S(6)} %copy.13.prefix_ref, s32[1]{0:T(128)S(6)} %copy.14.slen_ref, bf16[64,576]{1,0:T(8,128)(2,1)S(1)} %bitcast.10, bf16[16,576]{1,0:T(8,128)(2,1)S(1)} %bitcast.13, ...), custom_call_target="tpu_custom_call" | custom-call | tf_op jit(solution)/shard_map/gather_keys/pallas_call | solution.py:424
  42.0 0.0 copy-done.6
  42.0 16.9 %attend.1 = (bf16[2048,512]{1,0:T(8,128)(2,1)}, bf16[64,512]{1,0:T(8,128)(2,1)}, bf16[2,576]{1,0:T(2,128)(2,1)}) custom-call(s32[1]{0:T(128)S(6)} %copy.13.prefix_ref, s32[1]{0:T(128)S(6)} %copy.14.slen_ref, bf16[2560,640]{1,0:T(8,128)(2,1)S(1)} %get-tuple-element.9.key_ref, bf16[2112,640]{1,0:T(8,128)(2,1)S(1)} %get-tuple-element.10.qa_ref, ...), custom_call_target="tpu_custom_call" | custom-call | tf_op jit(solution)/shard_map/attend/pallas_call | solution.py:459
Async XLA Ops:
  0.6 41.4 %copy-start.6 = (f32[512]{0:T(512)S(1)}, f32[512]{0:T(512)}, u32[]{:S(2)}) copy-start(f32[512]{0:T(512)} %param.18) | copy-start | bytes 6148
  1.9 1.7 %copy-start = (bf16[1,64,32,576]{3,2,1,0:T(8,128)(2,1)S(1)}, bf16[1,64,32,576]{3,2,1,0:T(8,128)(2,1)}, u32[]{:S(2)}) copy-start(bf16[1,64,32,576]{3,2,1,0:T(8,128)(2,1)} %param.15) | copy-start | bytes 7077892
  3.7 0.9 %copy-start.1 = (bf16[112,576]{1,0:T(8,128)(2,1)S(1)}, bf16[112,576]{1,0:T(8,128)(2,1)}, u32[]{:S(2)}) copy-start(bf16[112,576]{1,0:T(8,128)(2,1)} %down_ref.1) | copy-start | bytes 387076
  4.6 0.9 %copy-start.2 = (bf16[1,64,576]{2,1,0:T(8,128)(2,1)S(1)}, bf16[1,64,576]{2,1,0:T(8,128)(2,1)}, u32[]{:S(2)}) copy-start(bf16[1,64,576]{2,1,0:T(8,128)(2,1)} %param.14) | copy-start | bytes 221188
  5.5 0.9 %copy-start.3 = (bf16[1,2,32,576]{3,2,1,0:T(8,128)(2,1)S(1)}, bf16[1,2,32,576]{3,2,1,0:T(8,128)(2,1)}, u32[]{:S(2)}) copy-start(bf16[1,2,32,576]{3,2,1,0:T(8,128)(2,1)} %param.19) | copy-start | bytes 221188
  6.4 0.7 %copy-start.4 = (bf16[1,2,7168]{2,1,0:T(2,128)(2,1)S(1)}, bf16[1,2,7168]{2,1,0:T(2,128)(2,1)}, u32[]{:S(2)}) copy-start(bf16[1,2,7168]{2,1,0:T(2,128)(2,1)} %param.16) | copy-start | bytes 86020
  7.1 0.7 %copy-start.5 = (bf16[1,1,16,576]{3,2,1,0:T(8,128)(2,1)S(1)}, bf16[1,1,16,576]{3,2,1,0:T(8,128)(2,1)}, u32[]{:S(2)}) copy-start(bf16[1,1,16,576]{3,2,1,0:T(8,128)(2,1)} %param.10) | copy-start | bytes 55300
  7.8 0.7 %copy-start.7 = (s32[1,32]{1,0:T(1,128)S(1)}, s32[1,32]{1,0:T(1,128)}, u32[]{:S(2)}) copy-start(s32[1,32]{1,0:T(1,128)} %hits_ref.1) | copy-start | bytes 388

commit v2 on v0

v2 whole, which is shorter than its diff:
```python
import jax
import jax.numpy as jnp
from jax import lax
from jax.experimental import pallas as pl
from jax.experimental.pallas import tpu as pltpu
from jax.sharding import PartitionSpec as P

SCALE2 = 192.0 ** (-0.5) * 1.4426950408889634
BIG = -1e38
MESH = pl.DeviceIdType.MESH
DIMS = (((1,), (1,)), ((), ()))

NX, NY = 4, 8
TOK, HEADS, KVW, LAT, WIDE = 64, 32, 576, 512, 640
ROWS = TOK * HEADS
DROWS = 2 * HEADS
CHUNK = 80
KEYS = NX * NY * CHUNK

SEGMENTS = (
    (0, 0), (0, 1), (1, 0), (2, 0), (0, 2), (3, 0), (1, 1), (2, 1), (0, 3), (0, 4),
    (1, 2), (2, 2), (3, 1), (1, 3), (2, 3), (3, 2), (1, 4), (2, 4), (3, 3), (3, 4),
)


def pair(u):
    return 1 <= u <= 3


def first_chunks():
    place, at = {}, 0
    for g, u in SEGMENTS:
        place[g, u] = at
        at += 2 if pair(u) else 1
    return place


FIRST = first_chunks()
SEM_Y, SEM_X1, SEM_X2, SEM_FAR, SEM_CORE, SEMS = 0, 5, 10, 15, 20, 40

ROW_BLOCKS = ((0, 512), (512, 512), (1024, 512), (1536, 512 + DROWS))
KEY_BLOCKS = ((0, 256), (256, 256), (512, 512), (1024, 512), (1536, 512), (2048, 512))
TALL, BROAD, SUB = 512 + DROWS, 512, 256

SERVICE = {
    (0, 1): (("ready", 2),),
    (0, 3): (("sum",), ("far", 0)),
    (1, 1): (("near", 1), ("ready", 3)),
    (1, 3): (("sum",),),
    (2, 0): (("ready", 4),),
    (2, 1): (("near", 2),),
    (2, 2): (("far", 1),),
    (2, 3): (("sum",),),
    (3, 0): (("near", 3),),
    (3, 1): (("far", 2), ("sum",)),
    (3, 2): (("near", 4),),
    (3, 3): (("sum",),),
    (4, 0): (("far", 3),),
    (4, 1): (("far", 4),),
}


def needed(block):
    start, width = KEY_BLOCKS[block]
    out = []
    for g, u in SEGMENTS:
        low = FIRST[g, u] * CHUNK
        high = low + (2 if pair(u) else 1) * CHUNK
        if low < start + width and high > start:
            out.append((g, u))
    return out


def fused_kernel(
    prefix_ref,
    slen_ref,
    hits_hbm,
    suffix_hbm,
    cache_hbm,
    hidden_hbm,
    down_hbm,
    dq_hbm,
    q_hbm,
    gain_hbm,
    out_ref,
    dec_ref,
    fresh_ref,
    gain_ref,
    hits_ref,
    suffix_ref,
    cache_ref,
    hidden_ref,
    down_ref,
    dq_ref,
    q_in,
    key_ref,
    qa_ref,
    acc_ref,
    m_ref,
    l_ref,
    s0,
    s1,
    p0,
    p1,
    part_send,
    part_recv,
    send_sem,
    recv_sem,
    psend_sem,
    precv_sem,
    in_sem,
):
    pool = lax.axis_index("pool")
    ctx = lax.axis_index("context")
    core = lax.axis_index("tensor")
    x, y = ctx // NY, ctx % NY

    def chip(dx, dy):
        return (pool, ((x + dx + NX) % NX) * NY + (y + dy + NY) % NY, core)

    sister = (pool, ctx, 1 - core)
    along = 1 - 2 * core
    fold = [
        sister,
        (pool, (x + 1 - 2 * (x % 2)) * NY + y, core),
        (pool, (NX - 1 - x) * NY + y, core),
        (pool, x * NY + y + 1 - 2 * (y % 2), core),
        (pool, x * NY + y + 2 - 4 * ((y // 2) % 2), core),
        chip(0, 4),
    ]
    friends = [sister, chip(1, 0), chip(-1, 0), chip(0, 1), chip(0, -1), chip(0, 2), chip(0, -2), chip(0, 4)]
    barrier = pltpu.get_barrier_semaphore()
    for friend in friends:
        pl.semaphore_signal(barrier, inc=1, device_id=friend, device_id_type=MESH)

    loads = (
        (suffix_hbm, suffix_ref),
        (cache_hbm, cache_ref),
        (hits_hbm, hits_ref),
        (hidden_hbm, hidden_ref),
        (down_hbm, down_ref),
        (dq_hbm, dq_ref),
        (q_hbm, q_in),
        (gain_hbm, gain_ref),
    )
    loads = [pltpu.make_async_copy(a, b, in_sem.at[i]) for i, (a, b) in enumerate(loads)]
    for load in loads:
        load.start()

    for load in loads[0:3]:
        load.wait()
    prefix = prefix_ref[0]
    slen = slen_ref[0]
    lane = lax.broadcasted_iota(jnp.int32, (TOK, TOK), 1)
    token = lax.broadcasted_iota(jnp.int32, (TOK, TOK), 0) + ctx * TOK
    hidden_here = ((lane < 32) & (ctx > lane)) | ((lane == 32) & (token >= slen))
    tail = jnp.where(hidden_here, BIG, 0.0).astype(jnp.bfloat16)
    key_ref[0:TOK, :] = jnp.concatenate([suffix_ref[...], tail], axis=1)
    order = lax.broadcasted_iota(jnp.int32, (1, 32), 1)
    hit = jnp.where((hits_ref[...] == ctx) & (order < prefix), 1.0, 0.0)
    live = jnp.max(hit, axis=1, keepdims=True)
    dead = jnp.broadcast_to(jnp.where(live > 0.5, 0.0, BIG), (16, TOK)).astype(jnp.bfloat16)
    key_ref[TOK:CHUNK, :] = jnp.concatenate([cache_ref[...], dead], axis=1)

    for load in loads[3:5]:
        load.wait()
    part = ctx * 2 + core
    lane_block = jnp.minimum((part * 112) // 128, 54)
    shift = part * 112 - lane_block * 128
    window = hidden_ref[:, pl.ds(pl.multiple_of(lane_block * 128, 128), 256)]
    pick = lax.broadcasted_iota(jnp.int32, (256, 112), 0) == lax.broadcasted_iota(jnp.int32, (256, 112), 1) + shift
    pick = jnp.where(pick, 1.0, 0.0).astype(jnp.bfloat16)
    piece = jnp.dot(window, pick, preferred_element_type=jnp.float32).astype(jnp.bfloat16)
    partial = jnp.dot(piece, down_ref[...], preferred_element_type=jnp.float32)
    part_send[...] = jnp.zeros_like(part_send)
    part_send[0, 0:2, 0:KVW] = partial

    pl.semaphore_wait(barrier, len(friends))

    def rows_of(g, u, of_core):
        if pair(u):
            return pl.ds(pl.multiple_of(FIRST[g, u] * CHUNK + of_core * CHUNK, 16), CHUNK)
        return pl.ds(FIRST[g, u] * CHUNK, CHUNK)

    def remote(source, target, i, device, of_core=None):
        of_core = core if of_core is None else of_core
        return pltpu.make_async_remote_copy(
            src_ref=key_ref.at[rows_of(*source, of_core)],
            dst_ref=key_ref.at[rows_of(*target, of_core)],
            send_sem=send_sem.at[i],
            recv_sem=recv_sem.at[i],
            device_id=device,
            device_id_type=MESH,
        )

    def y_copy(u, source, hops):
        return remote((0, source), (0, u), SEM_Y + u, chip(0, along * hops))

    def y_first(u):
        return pltpu.make_async_remote_copy(
            src_ref=key_ref.at[pl.ds(0, CHUNK)],
            dst_ref=key_ref.at[rows_of(0, u, core)],
            send_sem=send_sem.at[SEM_Y + u],
            recv_sem=recv_sem.at[SEM_Y + u],
            device_id=chip(0, along * u),
            device_id_type=MESH,
        )

    def x1_copy(u):
        return remote((0, u), (1, u), SEM_X1 + u, chip(1, 0))

    def x2_copy(u):
        return remote((0, u), (2, u), SEM_X2 + u, chip(-1, 0))

    def far_copy(u):
        if u % 2 == 0:
            return remote((1, u), (3, u), SEM_FAR + u, chip(1, 0))
        return remote((2, u), (3, u), SEM_FAR + u, chip(-1, 0))

    def core_copy(g, u, of_core=None):
        return remote((g, u), (g, u), SEM_CORE + g * 5 + u, sister, of_core)

    def carried(u, action):
        if u == 0:
            pl.when(core == 1)(action)
        elif u == 4:
            pl.when(core == 0)(action)
        else:
            action()

    def y_wait(u):
        if u == 4:
            return y_copy(4, 2, 2)
        if u == 3:
            return y_copy(3, 1, 2)
        return y_first(u)

    def ready(u):
        if u > 0:
            carried(u, lambda: y_wait(u).wait_recv())
        if u == 1:
            y_copy(3, 1, 2).start()
        if u == 2:
            pl.when(core == 0)(lambda: y_copy(4, 2, 2).start())

        def send():
            x1_copy(u).start()
            x2_copy(u).start()
            if u > 0:
                core_copy(0, u).start()

        carried(u, send)

    def near(u):
        def pass_on():
            x1_copy(u).wait_recv()
            if u % 2 == 0:
                far_copy(u).start()
            core_copy(1, u).start()
            x2_copy(u).wait_recv()
            if u % 2 == 1:
                far_copy(u).start()
            core_copy(2, u).start()

        carried(u, pass_on)

    def far(u):
        def pass_on():
            far_copy(u).wait_recv()
            core_copy(3, u).start()

        carried(u, pass_on)

    def fold_copy(i):
        return pltpu.make_async_remote_copy(
            src_ref=part_send.at[i],
            dst_ref=part_recv.at[i],
            send_sem=psend_sem.at[i],
            recv_sem=precv_sem.at[i],
            device_id=fold[i],
            device_id_type=MESH,
        )

    def fold_step(i):
        if i > 0:
            fold_copy(i - 1).wait_recv()
            part_send[i] = part_send[i - 1] + part_recv[i - 1]
        if i < 6:
            fold_copy(i).start()

    sums = [0]
    arrived = {(0, 0)}
    served = {(0, 0)}

    def serve(event):
        kind = event[0]
        if kind == "sum":
            fold_step(sums[0])
            sums[0] += 1
        elif kind == "ready":
            ready(event[1])
            served.add((0, event[1]))
        elif kind == "near":
            near(event[1])
            served.update({(1, event[1]), (2, event[1])})
        else:
            far(event[1])
            served.add((3, event[1]))

    def from_sister(g, u):
        def wait():
            core_copy(g, u, 1 - core).wait_recv()

        if u == 0:
            pl.when(core == 0)(wait)
        elif u == 4:
            pl.when(core == 1)(wait)
        else:
            wait()

    def await_block(block):
        for segment in needed(block):
            if segment not in arrived:
                assert segment in served, segment
                from_sister(*segment)
                arrived.add(segment)

    units = [(k, r) for k in range(len(KEY_BLOCKS)) for r in range(len(ROW_BLOCKS))]
    score, weight = [s0, s1], [p0, p1]
    last = len(KEY_BLOCKS) - 1

    def scores(i, j):
        k, r = units[i]
        start, n = ROW_BLOCKS[r]
        low = KEY_BLOCKS[k][0] + j * SUB
        s = lax.dot_general(qa_ref[start : start + n, :], key_ref[low : low + SUB, :], DIMS, preferred_element_type=jnp.float32)
        if low == 0:
            row = lax.broadcasted_iota(jnp.int32, (n, 128), 0)
            col = lax.broadcasted_iota(jnp.int32, (n, 128), 1)
            tok = (row + start) // HEADS
            mask = (col < TOK) & (col > tok) & (tok < TOK)
            score[i % 2][0:n, 0:128] = jnp.where(mask, BIG, s[:, 0:128])
            score[i % 2][0:n, 128:SUB] = s[:, 128:]
        else:
            score[i % 2][0:n, j * SUB : (j + 1) * SUB] = s

    def subs(i):
        return range(KEY_BLOCKS[units[i][0]][1] // SUB)

    def row_max(i):
        k, r = units[i]
        start, n = ROW_BLOCKS[r]
        top = jnp.max(score[i % 2][0:n, 0 : KEY_BLOCKS[k][1]], axis=1, keepdims=True) * SCALE2
        if k == 0:
            m_ref[start : start + n] = top
            return None
        old = m_ref[start : start + n]
        new = jnp.maximum(old, top)
        m_ref[start : start + n] = new
        return jnp.exp2(old - new)

    def soft(i, j, total):
        k, r = units[i]
        start, n = ROW_BLOCKS[r]
        s = score[i % 2][0:n, j * SUB : (j + 1) * SUB]
        p = jnp.exp2(s * SCALE2 - m_ref[start : start + n])
        weight[i % 2][0:n, j * SUB : (j + 1) * SUB] = p.astype(jnp.bfloat16)
        return total + jnp.sum(p, axis=1, keepdims=True)

    def fresh_rows():
        raw = part_send[6]
        latent = raw[:, 0:LAT]
        norm = latent * lax.rsqrt(jnp.sum(latent * latent, axis=1, keepdims=True) * (1.0 / LAT) + 1e-06) * gain_ref[...]
        rope = raw[:, LAT:WIDE]
        lanes = lax.broadcasted_iota(jnp.int32, (8, 128), 1)
        step = lax.broadcasted_iota(jnp.int32, (8, 128), 0)
        pos = (prefix * 16 + slen + step).astype(jnp.float32)
        freq = jnp.exp((lanes % 32).astype(jnp.float32) * (-9.210340371976184 / 32.0))
        angle = pos * freq
        cosine, sine = jnp.cos(angle), jnp.sin(angle)
        ahead = pltpu.roll(rope, 96, 1)
        behind = pltpu.roll(rope, 32, 1)
        turned = jnp.where(lanes < 32, rope * cosine - ahead * sine, rope * cosine + behind * sine)
        turned = jnp.where(lanes < 64, turned, 0.0)
        return jnp.concatenate([norm, turned], axis=1).astype(jnp.bfloat16)

    def decode_end(acc, total):
        fresh = fresh_rows()
        fresh_ref[...] = fresh[0:2, 0:KVW]
        sf = lax.dot_general(qa_ref[ROWS : ROWS + DROWS, :], fresh, DIMS, preferred_element_type=jnp.float32) * SCALE2
        row = lax.broadcasted_iota(jnp.int32, (DROWS, 8), 0) // HEADS
        col = lax.broadcasted_iota(jnp.int32, (DROWS, 8), 1)
        sf = jnp.where(col <= row, sf, BIG)
        old = m_ref[ROWS : ROWS + DROWS]
        new = jnp.maximum(old, jnp.max(sf, axis=1, keepdims=True))
        pf = jnp.exp2(sf - new)
        fade = jnp.exp2(old - new)
        total = total * fade + jnp.sum(pf, axis=1, keepdims=True)
        more = jnp.dot(pf.astype(jnp.bfloat16), fresh[:, 0:LAT], preferred_element_type=jnp.float32)
        dec_ref[...] = ((acc * fade + more) / total).astype(jnp.bfloat16)

    def context(i, total, fade):
        k, r = units[i]
        start, n = ROW_BLOCKS[r]
        low, width = KEY_BLOCKS[k]
        o = jnp.dot(weight[i % 2][0:n, 0:width], key_ref[low : low + width, 0:LAT], preferred_element_type=jnp.float32)
        here = slice(start, start + n)
        if k > 0:
            total = l_ref[here] * fade + total
            o = acc_ref[here] * fade + o
        if k < last:
            l_ref[here] = total
            acc_ref[here] = o
            return
        end = min(start + n, ROWS) - start
        out_ref[start : start + end, :] = (o[0:end] / total[0:end]).astype(jnp.bfloat16)
        if end < n:
            decode_end(o[end:n], total[end:n])

    y_first(1).start()
    pl.when(core == 0)(lambda: y_first(2).start())

    def own_step():
        pltpu.make_async_remote_copy(
            src_ref=key_ref.at[pl.ds(0, CHUNK)],
            dst_ref=key_ref.at[rows_of(0, 2, core)],
            send_sem=send_sem.at[SEM_Y + 2],
            recv_sem=recv_sem.at[SEM_Y + 2],
            device_id=chip(0, -2),
            device_id_type=MESH,
        ).start()

    pl.when(core == 1)(own_step)
    ready(0)
    serve(("sum",))

    for load in loads[5:]:
        load.wait()
    lanes = lax.broadcasted_iota(jnp.int32, (256, TOK), 1)
    pick_rank = jnp.where(lanes == ctx, 1.0, 0.0).astype(jnp.bfloat16)

    def widen(i, carry):
        rows = pl.ds(pl.multiple_of(i * 256, 256), 256)
        qa_ref[rows, :] = jnp.concatenate([q_in[rows, :], pick_rank], axis=1)
        return carry

    lax.fori_loop(0, ROWS // 256, widen, 0)
    pick_dec = jnp.where(lanes[0:DROWS] == 32, 1.0, 0.0).astype(jnp.bfloat16)
    qa_ref[ROWS : ROWS + DROWS, :] = jnp.concatenate([dq_ref[...], pick_dec], axis=1)

    for event in (("ready", 1), ("near", 0), ("sum",)):
        serve(event)

    await_block(0)
    for j in subs(0):
        scores(0, j)
    fade = row_max(0)
    for i, unit in enumerate(units):
        more = i + 1 < len(units)
        if more and units[i + 1][0] != unit[0]:
            await_block(units[i + 1][0])
        total = 0.0
        ahead = list(subs(i + 1)) if more else []
        for j in range(max(len(ahead), len(subs(i)))):
            if j < len(ahead):
                scores(i + 1, j)
            if j < len(subs(i)):
                total = soft(i, j, total)
        context(i, total, fade)
        if more:
            fade = row_max(i + 1)
        for event in SERVICE.get(unit, ()):
            serve(event)

    assert sums[0] == 7
    y_first(1).wait_send()
    y_copy(3, 1, 2).wait_send()
    y_first(2).wait_send()
    pl.when(core == 0)(lambda: y_copy(4, 2, 2).wait_send())
    for u in range(5):

        def sent(u=u):
            for copy in (x1_copy(u), x2_copy(u), far_copy(u)):
                copy.wait_send()
            for g in range(4):
                if (g, u) != (0, 0):
                    core_copy(g, u).wait_send()

        carried(u, sent)
    for i in range(6):
        fold_copy(i).wait_send()


def on_device(
    cache,
    hit_slots,
    prefix_blocks,
    suffix_len,
    suffix_latent,
    suffix_query,
    decode_hidden,
    kv_down,
    kv_gain,
    decode_query,
):
    vmem = pl.BlockSpec(memory_space=pltpu.VMEM)
    smem = pl.BlockSpec(memory_space=pltpu.SMEM)
    hbm = pl.BlockSpec(memory_space=pltpu.HBM)
    bf16, f32 = jnp.bfloat16, jnp.float32
    out, dec, fresh = pl.pallas_call(
        fused_kernel,
        name="attend",
        in_specs=[smem, smem] + [hbm] * 8,
        out_specs=[vmem, vmem, vmem],
        out_shape=[
            pltpu.VMEM((ROWS, LAT), bf16),
            pltpu.VMEM((DROWS, LAT), bf16),
            pltpu.VMEM((2, KVW), bf16),
        ],
        scratch_shapes=[
            pltpu.VMEM((1, LAT), f32),
            pltpu.VMEM((1, 32), jnp.int32),
            pltpu.VMEM((TOK, KVW), bf16),
            pltpu.VMEM((16, KVW), bf16),
            pltpu.VMEM((2, 7168), bf16),
            pltpu.VMEM((112, KVW), bf16),
            pltpu.VMEM((DROWS, KVW), bf16),
            pltpu.VMEM((ROWS, KVW), bf16),
            pltpu.VMEM((KEYS, WIDE), bf16),
            pltpu.VMEM((ROWS + DROWS, WIDE), bf16),
            pltpu.VMEM((ROWS + DROWS, LAT), f32),
            pltpu.VMEM((ROWS + DROWS, 1), f32),
            pltpu.VMEM((ROWS + DROWS, 1), f32),
            pltpu.VMEM((TALL, BROAD), f32),
            pltpu.VMEM((TALL, BROAD), f32),
            pltpu.VMEM((TALL, BROAD), bf16),
            pltpu.VMEM((TALL, BROAD), bf16),
            pltpu.VMEM((7, 8, WIDE), f32),
            pltpu.VMEM((6, 8, WIDE), f32),
            pltpu.SemaphoreType.DMA((SEMS,)),
            pltpu.SemaphoreType.DMA((SEMS,)),
            pltpu.SemaphoreType.DMA((6,)),
            pltpu.SemaphoreType.DMA((6,)),
            pltpu.SemaphoreType.DMA((8,)),
        ],
        compiler_params=pltpu.CompilerParams(
            collective_id=0, has_side_effects=True, vmem_limit_bytes=48 * 2**20
        ),
    )(
        prefix_blocks,
        suffix_len,
        *(
            pltpu.with_memory_space_constraint(array, pltpu.HBM)
            for array in (
                hit_slots,
                suffix_latent[0],
                cache[0, 0],
                decode_hidden[0],
                kv_down,
                decode_query.reshape(DROWS, KVW),
                suffix_query.reshape(ROWS, KVW),
                kv_gain.reshape(1, LAT),
            )
        ),
    )
    return (
        out.reshape(1, TOK, HEADS, LAT),
        dec.reshape(1, 2, HEADS, LAT),
        fresh.reshape(1, 2, KVW),
    )


def solution(mesh):
    placed = (
        P("pool", "context", None, None),
        P("pool", None),
        P("pool"),
        P("pool"),
        P("pool", "context", None),
        P("pool", "context", "tensor", None),
        P("pool", None, None),
        P(("context", "tensor"), None),
        P(),
        P("pool", None, "tensor", None),
    )
    return jax.shard_map(
        on_device,
        mesh=mesh,
        in_specs=placed,
        out_specs=(
            P("pool", "context", "tensor", None),
            P("pool", None, "tensor", None),
            P("pool", None, None),
        ),
        check_vma=False,
    )
```

time: 294 us -> 48.9 us (0.17)
  the two profiles are of different devices: /device:TPU:2 before, /device:TPU:1 now
where the time goes in v2:
time: 48.9 us; the launch traced here: 48.7 us
  Pallas kernels  44.2 us (90%)
  local copies, waits for them, and re-layouts  2.53 us (5%)
  between operations  1.93 us (4%)
    pallas_call x1, Pallas kernels, on_device(): pl.pallas_call(fused_kernel, name='attend', in_specs=[smem, smem] + [hbm]...  44.2 us
    unnamed x3, local copies, waits for them, and re-layouts  2.53 us

profile of v2, /device:TPU:1, one launch (start us, length us, event | category | flops | bytes accessed | tf_op | source)
XLA Modules:
  0.0 48.7 jit_solution(8450758942402293337)
XLA Ops:
  1.9 44.2 %attend.1 = (bf16[2048,512]{1,0:T(8,128)(2,1)S(1)}, bf16[64,512]{1,0:T(8,128)(2,1)S(1)}, bf16[2,576]{1,0:T(2,128)(2,1)S(1)}) custom-call(s32[1]{0:T(128)S(6)} %copy.19.prefix_ref, s32[1]{0:T(128)S(6)} %copy.20.slen_ref, s32[1,32]{1,0:T(1,128)} %hits_hbm.1, bf16[64,576]{1,0:T(8,128)(2,1)} %bitcast.13, bf16[16,576]{1,0:T(8,128)(2,1)} %bitcast.16, ...), custom_call_target="tpu_custom_call" | custom-call | tf_op jit(solution)/shard_map/attend/pallas_call | solution.py:510
  46.2 1.3 %copy.16 = bf16[1,64,32,512]{3,2,1,0:T(8,128)(2,1)} copy(bf16[1,64,32,512]{3,2,1,0:T(8,128)(2,1)S(1)} %bitcast.9) | data formatting | bytes 4194304
  47.5 0.6 %copy.17 = bf16[1,2,32,512]{3,2,1,0:T(8,128)(2,1)} copy(bf16[1,2,32,512]{3,2,1,0:T(8,128)(2,1)S(1)} %bitcast.10) | data formatting | bytes 131072
  48.1 0.6 %copy.18 = bf16[1,2,576]{2,1,0:T(2,128)(2,1)} copy(bf16[1,2,576]{2,1,0:T(2,128)(2,1)S(1)} %bitcast.11) | data formatting | bytes 4608

commit v3 on v2

--- a/solution.py
+++ b/solution.py
@@ -19,8 +19,9 @@
 
 SEGMENTS = (
     (0, 0), (0, 1), (1, 0), (2, 0), (0, 2), (3, 0), (1, 1), (2, 1), (0, 3), (0, 4),
-    (1, 2), (2, 2), (3, 1), (1, 3), (2, 3), (3, 2), (1, 4), (2, 4), (3, 3), (3, 4),
+    (1, 2), (2, 2), (3, 1), (3, 2), (1, 3), (2, 3), (3, 3), (1, 4), (2, 4), (3, 4),
 )
+CARRIER = {(0, 4): 0, (1, 4): 0, (2, 4): 0, (3, 4): 0, (1, 0): 0, (2, 0): 1, (3, 0): 0, (3, 1): 0}
 
 
 def pair(u):
@@ -36,27 +37,25 @@
 
 
 FIRST = first_chunks()
-SEM_Y, SEM_X1, SEM_X2, SEM_FAR, SEM_CORE, SEMS = 0, 5, 10, 15, 20, 40
+SEM_Y, SEM_X1, SEM_X2, SEM_FAR, SEM_CORE, SEM_SIDE, SEMS = 0, 5, 10, 15, 20, 40, 42
 
 ROW_BLOCKS = ((0, 512), (512, 512), (1024, 512), (1536, 512 + DROWS))
-KEY_BLOCKS = ((0, 256), (256, 256), (512, 512), (1024, 512), (1536, 512), (2048, 512))
+KEY_BLOCKS = ((0, 256), (256, 256), (512, 512), (1024, 512), (1536, 512), (2048, 256), (2304, 256))
 TALL, BROAD, SUB = 512 + DROWS, 512, 256
 
 SERVICE = {
     (0, 1): (("ready", 2),),
-    (0, 3): (("sum",), ("far", 0)),
-    (1, 1): (("near", 1), ("ready", 3)),
-    (1, 3): (("sum",),),
-    (2, 0): (("ready", 4),),
-    (2, 1): (("near", 2),),
-    (2, 2): (("far", 1),),
+    (0, 3): (("far", 0),),
+    (1, 0): (("sum",),),
+    (1, 1): (("ready", 3), ("near", 1)),
+    (2, 0): (("ready", 4), ("near", 2)),
+    (2, 1): (("side",), ("sum",)),
     (2, 3): (("sum",),),
-    (3, 0): (("near", 3),),
-    (3, 1): (("far", 2), ("sum",)),
-    (3, 2): (("near", 4),),
+    (3, 1): (("far", 2),),
+    (3, 2): (("near", 3), ("far", 3)),
     (3, 3): (("sum",),),
-    (4, 0): (("far", 3),),
-    (4, 1): (("far", 4),),
+    (4, 0): (("near", 4), ("far", 4)),
+    (4, 3): (("sum",),),
 }
 
 
@@ -128,7 +127,7 @@
         (pool, x * NY + y + 2 - 4 * ((y // 2) % 2), core),
         chip(0, 4),
     ]
-    friends = [sister, chip(1, 0), chip(-1, 0), chip(0, 1), chip(0, -1), chip(0, 2), chip(0, -2), chip(0, 4)]
+    friends = [sister, chip(1, 0), chip(-1, 0), chip(2, 0), chip(0, 1), chip(0, -1), chip(0, 2), chip(0, -2), chip(0, 4)]
     barrier = pltpu.get_barrier_semaphore()
     for friend in friends:
         pl.semaphore_signal(barrier, inc=1, device_id=friend, device_id_type=MESH)
@@ -162,19 +161,6 @@
     dead = jnp.broadcast_to(jnp.where(live > 0.5, 0.0, BIG), (16, TOK)).astype(jnp.bfloat16)
     key_ref[TOK:CHUNK, :] = jnp.concatenate([cache_ref[...], dead], axis=1)
 
-    for load in loads[3:5]:
-        load.wait()
-    part = ctx * 2 + core
-    lane_block = jnp.minimum((part * 112) // 128, 54)
-    shift = part * 112 - lane_block * 128
-    window = hidden_ref[:, pl.ds(pl.multiple_of(lane_block * 128, 128), 256)]
-    pick = lax.broadcasted_iota(jnp.int32, (256, 112), 0) == lax.broadcasted_iota(jnp.int32, (256, 112), 1) + shift
-    pick = jnp.where(pick, 1.0, 0.0).astype(jnp.bfloat16)
-    piece = jnp.dot(window, pick, preferred_element_type=jnp.float32).astype(jnp.bfloat16)
-    partial = jnp.dot(piece, down_ref[...], preferred_element_type=jnp.float32)
-    part_send[...] = jnp.zeros_like(part_send)
-    part_send[0, 0:2, 0:KVW] = partial
-
     pl.semaphore_wait(barrier, len(friends))
 
     def rows_of(g, u, of_core):
@@ -182,94 +168,101 @@
             return pl.ds(pl.multiple_of(FIRST[g, u] * CHUNK + of_core * CHUNK, 16), CHUNK)
         return pl.ds(FIRST[g, u] * CHUNK, CHUNK)
 
-    def remote(source, target, i, device, of_core=None):
-        of_core = core if of_core is None else of_core
+    def span(g, u):
+        return pl.ds(FIRST[g, u] * CHUNK, 2 * CHUNK if pair(u) else CHUNK)
+
+    def remote(source, target, i, device):
         return pltpu.make_async_remote_copy(
-            src_ref=key_ref.at[rows_of(*source, of_core)],
-            dst_ref=key_ref.at[rows_of(*target, of_core)],
+            src_ref=key_ref.at[source],
+            dst_ref=key_ref.at[target],
             send_sem=send_sem.at[i],
             recv_sem=recv_sem.at[i],
             device_id=device,
             device_id_type=MESH,
         )
 
-    def y_copy(u, source, hops):
-        return remote((0, source), (0, u), SEM_Y + u, chip(0, along * hops))
-
-    def y_first(u):
-        return pltpu.make_async_remote_copy(
-            src_ref=key_ref.at[pl.ds(0, CHUNK)],
-            dst_ref=key_ref.at[rows_of(0, u, core)],
-            send_sem=send_sem.at[SEM_Y + u],
-            recv_sem=recv_sem.at[SEM_Y + u],
-            device_id=chip(0, along * u),
-            device_id_type=MESH,
-        )
-
-    def x1_copy(u):
-        return remote((0, u), (1, u), SEM_X1 + u, chip(1, 0))
-
-    def x2_copy(u):
-        return remote((0, u), (2, u), SEM_X2 + u, chip(-1, 0))
+    def y_copy(u):
+        source, hops = (rows_of(0, 0, core), u) if u <= 2 else (rows_of(0, u - 2, core), 2)
+        return remote(source, rows_of(0, u, core), SEM_Y + u, chip(0, along * hops))
+
+    def near_copy(g, u):
+        base = SEM_X1 if g == 1 else SEM_X2
+        return remote(rows_of(0, u, core), rows_of(g, u, core), base + u, chip(1 if g == 1 else -1, 0))
 
     def far_copy(u):
-        if u % 2 == 0:
-            return remote((1, u), (3, u), SEM_FAR + u, chip(1, 0))
-        return remote((2, u), (3, u), SEM_FAR + u, chip(-1, 0))
+        if u == 0:
+            source, hops = rows_of(1, 0, core), 1
+        elif u == 2:
+            source, hops = rows_of(2, 2, core), -1
+        else:
+            source, hops = rows_of(0, u, core), 2
+        return remote(source, rows_of(3, u, core), SEM_FAR + u, chip(hops, 0))
+
+    def side_copy(way):
+        return remote(rows_of(3, 0, core), rows_of(3, 1, way), SEM_SIDE + way, chip(0, 1 - 2 * way))
 
     def core_copy(g, u, of_core=None):
-        return remote((g, u), (g, u), SEM_CORE + g * 5 + u, sister, of_core)
-
-    def carried(u, action):
+        if (g, u) in CARRIER or not pair(u):
+            rows = span(g, u)
+        else:
+            rows = rows_of(g, u, core if of_core is None else of_core)
+        return remote(rows, rows, SEM_CORE + g * 5 + u, sister)
+
+    def on(which, action):
+        if which is None:
+            action()
+        else:
+            pl.when(core == which)(action)
+
+    started = []
+
+    def launch(which, *copies):
+        def start():
+            for make in copies:
+                make().start()
+
+        on(which, start)
+        started.append((which, copies))
+
+    def take(g, u, *copies):
+        which = CARRIER.get((g, u))
+
+        def wait():
+            for make in copies:
+                make().wait_recv()
+
+        on(which, wait)
+        return which
+
+    def ready(u):
+        which = take(0, u, lambda: y_copy(u))
+        if u == 1:
+            launch(which, lambda: y_copy(3))
+        if u == 2:
+            launch(0, lambda: y_copy(4))
+        launch(which, lambda: near_copy(1, u), lambda: near_copy(2, u))
+        if u >= 3:
+            launch(which, lambda: far_copy(u))
+        launch(which, lambda: core_copy(0, u))
+
+    def near(u):
+        for g in (1, 2):
+            which = take(g, u, lambda g=g: near_copy(g, u))
+            if u == 0 and g == 1:
+                launch(which, lambda: far_copy(0))
+            if u == 2 and g == 2:
+                launch(which, lambda: far_copy(2))
+            launch(which, lambda g=g: core_copy(g, u))
+
+    def far(u):
+        which = take(3, u, lambda: far_copy(u))
         if u == 0:
-            pl.when(core == 1)(action)
-        elif u == 4:
-            pl.when(core == 0)(action)
-        else:
-            action()
-
-    def y_wait(u):
-        if u == 4:
-            return y_copy(4, 2, 2)
-        if u == 3:
-            return y_copy(3, 1, 2)
-        return y_first(u)
-
-    def ready(u):
-        if u > 0:
-            carried(u, lambda: y_wait(u).wait_recv())
-        if u == 1:
-            y_copy(3, 1, 2).start()
-        if u == 2:
-            pl.when(core == 0)(lambda: y_copy(4, 2, 2).start())
-
-        def send():
-            x1_copy(u).start()
-            x2_copy(u).start()
-            if u > 0:
-                core_copy(0, u).start()
-
-        carried(u, send)
-
-    def near(u):
-        def pass_on():
-            x1_copy(u).wait_recv()
-            if u % 2 == 0:
-                far_copy(u).start()
-            core_copy(1, u).start()
-            x2_copy(u).wait_recv()
-            if u % 2 == 1:
-                far_copy(u).start()
-            core_copy(2, u).start()
-
-        carried(u, pass_on)
-
-    def far(u):
-        def pass_on():
-            far_copy(u).wait_recv()
-            core_copy(3, u).start()
-
-        carried(u, pass_on)
+            launch(which, lambda: side_copy(0), lambda: side_copy(1))
+        launch(which, lambda: core_copy(3, u))
+
+    def side():
+        which = take(3, 1, lambda: side_copy(0), lambda: side_copy(1))
+        launch(which, lambda: core_copy(3, 1))
 
     def fold_copy(i):
         return pltpu.make_async_remote_copy(
@@ -303,20 +296,16 @@
         elif kind == "near":
             near(event[1])
             served.update({(1, event[1]), (2, event[1])})
-        else:
+        elif kind == "far":
             far(event[1])
             served.add((3, event[1]))
+        else:
+            side()
+            served.add((3, 1))
 
     def from_sister(g, u):
-        def wait():
-            core_copy(g, u, 1 - core).wait_recv()
-
-        if u == 0:
-            pl.when(core == 0)(wait)
-        elif u == 4:
-            pl.when(core == 1)(wait)
-        else:
-            wait()
+        which = CARRIER.get((g, u))
+        on(None if which is None else 1 - which, lambda: core_copy(g, u, 1 - core).wait_recv())
 
     def await_block(block):
         for segment in needed(block):
@@ -328,6 +317,9 @@
     units = [(k, r) for k in range(len(KEY_BLOCKS)) for r in range(len(ROW_BLOCKS))]
     score, weight = [s0, s1], [p0, p1]
     last = len(KEY_BLOCKS) - 1
+
+    def wide(state, lanes):
+        return jnp.concatenate([state] * (lanes // 128), axis=1)
 
     def scores(i, j):
         k, r = units[i]
@@ -351,6 +343,7 @@
         k, r = units[i]
         start, n = ROW_BLOCKS[r]
         top = jnp.max(score[i % 2][0:n, 0 : KEY_BLOCKS[k][1]], axis=1, keepdims=True) * SCALE2
+        top = jnp.broadcast_to(top, (n, 128))
         if k == 0:
             m_ref[start : start + n] = top
             return None
@@ -363,9 +356,11 @@
         k, r = units[i]
         start, n = ROW_BLOCKS[r]
         s = score[i % 2][0:n, j * SUB : (j + 1) * SUB]
-        p = jnp.exp2(s * SCALE2 - m_ref[start : start + n])
+        p = jnp.exp2(s * SCALE2 - wide(m_ref[start : start + n], SUB))
         weight[i % 2][0:n, j * SUB : (j + 1) * SUB] = p.astype(jnp.bfloat16)
-        return total + jnp.sum(p, axis=1, keepdims=True)
+        for c in range(0, SUB, 128):
+            total = p[:, c : c + 128] if total is None else total + p[:, c : c + 128]
+        return total
 
     def fresh_rows():
         raw = part_send[6]
@@ -391,7 +386,7 @@
         row = lax.broadcasted_iota(jnp.int32, (DROWS, 8), 0) // HEADS
         col = lax.broadcasted_iota(jnp.int32, (DROWS, 8), 1)
         sf = jnp.where(col <= row, sf, BIG)
-        old = m_ref[ROWS : ROWS + DROWS]
+        old = m_ref[ROWS : ROWS + DROWS, 0:1]
         new = jnp.maximum(old, jnp.max(sf, axis=1, keepdims=True))
         pf = jnp.exp2(sf - new)
         fade = jnp.exp2(old - new)
@@ -407,31 +402,36 @@
         here = slice(start, start + n)
         if k > 0:
             total = l_ref[here] * fade + total
-            o = acc_ref[here] * fade + o
+            o = acc_ref[here] * wide(fade, LAT) + o
         if k < last:
             l_ref[here] = total
             acc_ref[here] = o
             return
         end = min(start + n, ROWS) - start
-        out_ref[start : start + end, :] = (o[0:end] / total[0:end]).astype(jnp.bfloat16)
+        total = jnp.sum(total, axis=1, keepdims=True)
+        over = jnp.broadcast_to(1.0 / total[0:end], (end, 128))
+        out_ref[start : start + end, :] = (o[0:end] * wide(over, LAT)).astype(jnp.bfloat16)
         if end < n:
             decode_end(o[end:n], total[end:n])
 
-    y_first(1).start()
-    pl.when(core == 0)(lambda: y_first(2).start())
-
-    def own_step():
-        pltpu.make_async_remote_copy(
-            src_ref=key_ref.at[pl.ds(0, CHUNK)],
-            dst_ref=key_ref.at[rows_of(0, 2, core)],
-            send_sem=send_sem.at[SEM_Y + 2],
-            recv_sem=recv_sem.at[SEM_Y + 2],
-            device_id=chip(0, -2),
-            device_id_type=MESH,
-        ).start()
-
-    pl.when(core == 1)(own_step)
-    ready(0)
+    y_copy(1).start()
+    launch(0, lambda: near_copy(1, 0))
+    launch(1, lambda: near_copy(2, 0))
+
+    for load in loads[3:5]:
+        load.wait()
+    part = ctx * 2 + core
+    lane_block = jnp.minimum((part * 112) // 128, 54)
+    shift = part * 112 - lane_block * 128
+    window = hidden_ref[:, pl.ds(pl.multiple_of(lane_block * 128, 128), 256)]
+    pick = lax.broadcasted_iota(jnp.int32, (256, 112), 0) == lax.broadcasted_iota(jnp.int32, (256, 112), 1) + shift
+    pick = jnp.where(pick, 1.0, 0.0).astype(jnp.bfloat16)
+    piece = jnp.dot(window, pick, preferred_element_type=jnp.float32).astype(jnp.bfloat16)
+    partial = jnp.dot(piece, down_ref[...], preferred_element_type=jnp.float32)
+    part_send[...] = jnp.zeros_like(part_send)
+    part_send[0, 0:2, 0:KVW] = partial
+    y_copy(1).wait_send()
+    launch(None, lambda: y_copy(2))
     serve(("sum",))
 
     for load in loads[5:]:
@@ -459,7 +459,7 @@
         more = i + 1 < len(units)
         if more and units[i + 1][0] != unit[0]:
             await_block(units[i + 1][0])
-        total = 0.0
+        total = None
         ahead = list(subs(i + 1)) if more else []
         for j in range(max(len(ahead), len(subs(i)))):
             if j < len(ahead):
@@ -473,22 +473,24 @@
             serve(event)
 
     assert sums[0] == 7
-    y_first(1).wait_send()
-    y_copy(3, 1, 2).wait_send()
-    y_first(2).wait_send()
-    pl.when(core == 0)(lambda: y_copy(4, 2, 2).wait_send())
-    for u in range(5):
-
-        def sent(u=u):
-            for copy in (x1_copy(u), x2_copy(u), far_copy(u)):
-                copy.wait_send()
-            for g in range(4):
-                if (g, u) != (0, 0):
-                    core_copy(g, u).wait_send()
-
-        carried(u, sent)
+    for which, copies in started:
+
+        def sent(copies=copies):
+            for make in copies:
+                make().wait_send()
+
+        on(which, sent)
     for i in range(6):
         fold_copy(i).wait_send()
+
+
+def write_kernel(out_vmem, dec_vmem, fresh_vmem, out_ref, dec_ref, fresh_ref, sem):
+    copies = ((out_vmem, out_ref), (dec_vmem, dec_ref), (fresh_vmem, fresh_ref))
+    copies = [pltpu.make_async_copy(a, b, sem.at[i]) for i, (a, b) in enumerate(copies)]
+    for copy in copies:
+        copy.start()
+    for copy in copies:
+        copy.wait()
 
 
 def on_device(
@@ -529,8 +531,8 @@
             pltpu.VMEM((KEYS, WIDE), bf16),
             pltpu.VMEM((ROWS + DROWS, WIDE), bf16),
             pltpu.VMEM((ROWS + DROWS, LAT), f32),
-            pltpu.VMEM((ROWS + DROWS, 1), f32),
-            pltpu.VMEM((ROWS + DROWS, 1), f32),
+            pltpu.VMEM((ROWS + DROWS, 128), f32),
+            pltpu.VMEM((ROWS + DROWS, 128), f32),
             pltpu.VMEM((TALL, BROAD), f32),
             pltpu.VMEM((TALL, BROAD), f32),
             pltpu.VMEM((TALL, BROAD), bf16),
@@ -563,6 +565,18 @@
             )
         ),
     )
+    out, dec, fresh = pl.pallas_call(
+        write_kernel,
+        name="write",
+        in_specs=[vmem] * 3,
+        out_specs=[hbm] * 3,
+        out_shape=[
+            jax.ShapeDtypeStruct((ROWS, LAT), bf16),
+            jax.ShapeDtypeStruct((DROWS, LAT), bf16),
+            jax.ShapeDtypeStruct((2, KVW), bf16),
+        ],
+        scratch_shapes=[pltpu.SemaphoreType.DMA((3,))],
+    )(out, dec, fresh)
     return (
         out.reshape(1, TOK, HEADS, LAT),
         dec.reshape(1, 2, HEADS, LAT),

time: 48.9 us -> 50.6 us (1.035)
  Pallas kernels: 44.2 us -> 45.8 us
    pallas_call x0 -> x1, Pallas kernels: none -> 2.98 us  [on_device(): pl.pallas_call(write_kernel, name='write', in_specs=[vmem] * 3, out_specs...]
    pallas_call x1, Pallas kernels: 44.2 us -> 42.8 us  [on_device(): pl.pallas_call(fused_kernel, name='attend', in_specs=[smem, smem] + [hbm]...]
    unnamed x3 -> x6, local copies, waits for them, and re-layouts: 2.53 us -> 2.52 us
where the time goes in v3:
time: 50.6 us; the launch traced here: 50.4 us
  Pallas kernels  45.8 us (91%)
  local copies, waits for them, and re-layouts  2.52 us (5%)
  between operations  2.1 us (4%)
    pallas_call x1, Pallas kernels, on_device(): pl.pallas_call(fused_kernel, name='attend', in_specs=[smem, smem] + [hbm]...  42.8 us
    pallas_call x1, Pallas kernels, on_device(): pl.pallas_call(write_kernel, name='write', in_specs=[vmem] * 3, out_specs...  2.98 us
    unnamed x6, local copies, waits for them, and re-layouts  2.52 us

profile of v3, /device:TPU:1, one launch (start us, length us, event | category | flops | bytes accessed | tf_op | source)
XLA Modules:
  0.0 50.4 jit_solution(12721741329911611314)
XLA Ops:
  1.9 42.8 %attend.1 = (bf16[2048,512]{1,0:T(8,128)(2,1)S(1)}, bf16[64,512]{1,0:T(8,128)(2,1)S(1)}, bf16[2,576]{1,0:T(2,128)(2,1)S(1)}) custom-call(s32[1]{0:T(128)S(6)} %copy.13.prefix_ref, s32[1]{0:T(128)S(6)} %copy.14.slen_ref, s32[1,32]{1,0:T(1,128)} %hits_hbm.1, bf16[64,576]{1,0:T(8,128)(2,1)} %bitcast.10, bf16[16,576]{1,0:T(8,128)(2,1)} %bitcast.13, ...), custom_call_target="tpu_custom_call" | custom-call | tf_op jit(solution)/shard_map/attend/pallas_call | solution.py:512
  44.8 0.0 copy-start
  44.8 1.3 %copy-done = bf16[2048,512]{1,0:T(8,128)(2,1)} copy-done((bf16[2048,512]{1,0:T(8,128)(2,1)}, bf16[2048,512]{1,0:T(8,128)(2,1)S(1)}, u32[]{:S(2)}) %copy-start) | copy-done | bytes 2097176
  46.1 0.0 copy-start.1
  46.1 0.6 %copy-done.1 = bf16[64,512]{1,0:T(8,128)(2,1)} copy-done((bf16[64,512]{1,0:T(8,128)(2,1)}, bf16[64,512]{1,0:T(8,128)(2,1)S(1)}, u32[]{:S(2)}) %copy-start.1) | copy-done | bytes 65560
  46.7 0.0 copy-start.2
  46.7 0.6 %copy-done.2 = bf16[2,576]{1,0:T(2,128)(2,1)} copy-done((bf16[2,576]{1,0:T(2,128)(2,1)}, bf16[2,576]{1,0:T(2,128)(2,1)S(1)}, u32[]{:S(2)}) %copy-start.2) | copy-done | bytes 2328
  47.3 3.0 %write.1 = (bf16[2048,512]{1,0:T(8,128)(2,1)}, bf16[64,512]{1,0:T(8,128)(2,1)}, bf16[2,576]{1,0:T(2,128)(2,1)}) custom-call(bf16[2048,512]{1,0:T(8,128)(2,1)} %copy-done, bf16[64,512]{1,0:T(8,128)(2,1)} %copy-done.1, bf16[2,576]{1,0:T(2,128)(2,1)} %copy-done.2), custom_call_target="tpu_custom_call" | custom-call | tf_op jit(solution)/shard_map/write/pallas_call | solution.py:568
Async XLA Ops:
  44.8 1.3 %copy-start = (bf16[2048,512]{1,0:T(8,128)(2,1)}, bf16[2048,512]{1,0:T(8,128)(2,1)S(1)}, u32[]{:S(2)}) copy-start(bf16[2048,512]{1,0:T(8,128)(2,1)S(1)} %get-tuple-element.9.out_vmem) | copy-start | bytes 6291460
  46.1 0.6 %copy-start.1 = (bf16[64,512]{1,0:T(8,128)(2,1)}, bf16[64,512]{1,0:T(8,128)(2,1)S(1)}, u32[]{:S(2)}) copy-start(bf16[64,512]{1,0:T(8,128)(2,1)S(1)} %get-tuple-element.10.dec_vmem) | copy-start | bytes 196612
  46.7 0.6 %copy-start.2 = (bf16[2,576]{1,0:T(2,128)(2,1)}, bf16[2,576]{1,0:T(2,128)(2,1)S(1)}, u32[]{:S(2)}) copy-start(bf16[2,576]{1,0:T(2,128)(2,1)S(1)} %get-tuple-element.11.fresh_vmem) | copy-start | bytes 6916

commit v4 on v3

--- a/solution.py
+++ b/solution.py
@@ -19,7 +19,7 @@
 
 SEGMENTS = (
     (0, 0), (0, 1), (1, 0), (2, 0), (0, 2), (3, 0), (1, 1), (2, 1), (0, 3), (0, 4),
-    (1, 2), (2, 2), (3, 1), (3, 2), (1, 3), (2, 3), (3, 3), (1, 4), (2, 4), (3, 4),
+    (1, 2), (2, 2), (3, 1), (3, 2), (1, 3), (2, 3), (1, 4), (2, 4), (3, 3), (3, 4),
 )
 CARRIER = {(0, 4): 0, (1, 4): 0, (2, 4): 0, (3, 4): 0, (1, 0): 0, (2, 0): 1, (3, 0): 0, (3, 1): 0}
 
@@ -44,18 +44,17 @@
 TALL, BROAD, SUB = 512 + DROWS, 512, 256
 
 SERVICE = {
-    (0, 1): (("ready", 2),),
+    (0, 2): (("sum",), ("ready", 2)),
     (0, 3): (("far", 0),),
-    (1, 0): (("sum",),),
-    (1, 1): (("ready", 3), ("near", 1)),
-    (2, 0): (("ready", 4), ("near", 2)),
-    (2, 1): (("side",), ("sum",)),
-    (2, 3): (("sum",),),
-    (3, 1): (("far", 2),),
-    (3, 2): (("near", 3), ("far", 3)),
-    (3, 3): (("sum",),),
-    (4, 0): (("near", 4), ("far", 4)),
-    (4, 3): (("sum",),),
+    (1, 0): (("near", 1), ("ready", 3)),
+    (1, 2): (("near", 2),),
+    (2, 0): (("side",), ("sum",), ("ready", 4)),
+    (2, 2): (("near", 3),),
+    (3, 0): (("far", 2), ("sum",)),
+    (3, 2): (("near", 4),),
+    (4, 1): (("far", 3), ("sum",)),
+    (4, 2): (("far", 4),),
+    (6, 0): (("sum",),),
 }
 
 
@@ -193,7 +192,9 @@
         if u == 0:
             source, hops = rows_of(1, 0, core), 1
         elif u == 2:
-            source, hops = rows_of(2, 2, core), -1
+            source, hops = rows_of(1, 2, core), 1
+        elif u == 3:
+            source, hops = rows_of(2, 3, core), -1
         else:
             source, hops = rows_of(0, u, core), 2
         return remote(source, rows_of(3, u, core), SEM_FAR + u, chip(hops, 0))
@@ -241,17 +242,15 @@
         if u == 2:
             launch(0, lambda: y_copy(4))
         launch(which, lambda: near_copy(1, u), lambda: near_copy(2, u))
-        if u >= 3:
+        if u == 4:
             launch(which, lambda: far_copy(u))
         launch(which, lambda: core_copy(0, u))
 
     def near(u):
         for g in (1, 2):
             which = take(g, u, lambda g=g: near_copy(g, u))
-            if u == 0 and g == 1:
-                launch(which, lambda: far_copy(0))
-            if u == 2 and g == 2:
-                launch(which, lambda: far_copy(2))
+            if (u, g) in ((0, 1), (2, 1), (3, 2)):
+                launch(which, lambda: far_copy(u))
             launch(which, lambda g=g: core_copy(g, u))
 
     def far(u):
@@ -576,7 +575,7 @@
             jax.ShapeDtypeStruct((2, KVW), bf16),
         ],
         scratch_shapes=[pltpu.SemaphoreType.DMA((3,))],
-    )(out, dec, fresh)
+    )(*(pltpu.with_memory_space_constraint(array, pltpu.VMEM) for array in (out, dec, fresh)))
     return (
         out.reshape(1, TOK, HEADS, LAT),
         dec.reshape(1, 2, HEADS, LAT),

time: 50.6 us -> 42.5 us (0.84)
  the two profiles are of different devices: /device:TPU:1 before, /device:TPU:2 now
where the time goes in v4:
time: 42.5 us; the launch traced here: 42.2 us
  Pallas kernels  40.1 us (94%)
  between operations  2.09 us (5%)
    pallas_call x1, Pallas kernels, on_device(): pl.pallas_call(fused_kernel, name='attend', in_specs=[smem, smem] + [hbm]...  38.8 us
    pallas_call x1, Pallas kernels, on_device(): pl.pallas_call(write_kernel, name='write', in_specs=[vmem] * 3, out_specs...  1.35 us

profile of v4, /device:TPU:2, one launch (start us, length us, event | category | flops | bytes accessed | tf_op | source)
XLA Modules:
  0.0 42.2 jit_solution(18046652428035809063)
XLA Ops:
  1.9 38.8 %attend.1 = (bf16[2048,512]{1,0:T(8,128)(2,1)S(1)}, bf16[64,512]{1,0:T(8,128)(2,1)S(1)}, bf16[2,576]{1,0:T(2,128)(2,1)S(1)}) custom-call(s32[1]{0:T(128)S(6)} %copy.13.prefix_ref, s32[1]{0:T(128)S(6)} %copy.14.slen_ref, s32[1,32]{1,0:T(1,128)} %hits_hbm.1, bf16[64,576]{1,0:T(8,128)(2,1)} %bitcast.10, bf16[16,576]{1,0:T(8,128)(2,1)} %bitcast.13, ...), custom_call_target="tpu_custom_call" | custom-call | tf_op jit(solution)/shard_map/attend/pallas_call | solution.py:511
  40.7 1.4 %write.1 = (bf16[2048,512]{1,0:T(8,128)(2,1)}, bf16[64,512]{1,0:T(8,128)(2,1)}, bf16[2,576]{1,0:T(2,128)(2,1)}) custom-call(bf16[2048,512]{1,0:T(8,128)(2,1)S(1)} %get-tuple-element.9.out_vmem, bf16[64,512]{1,0:T(8,128)(2,1)S(1)} %get-tuple-element.10.dec_vmem, bf16[2,576]{1,0:T(2,128)(2,1)S(1)} %get-tuple-element.11.fresh_vmem), custom_call_target="tpu_custom_call" | custom-call | tf_op jit(solution)/shard_map/write/pallas_call | solution.py:567

commit v5 on v4

--- a/solution.py
+++ b/solution.py
@@ -18,8 +18,8 @@
 KEYS = NX * NY * CHUNK
 
 SEGMENTS = (
-    (0, 0), (0, 1), (1, 0), (2, 0), (0, 2), (3, 0), (1, 1), (2, 1), (0, 3), (0, 4),
-    (1, 2), (2, 2), (3, 1), (3, 2), (1, 3), (2, 3), (1, 4), (2, 4), (3, 3), (3, 4),
+    (0, 0), (1, 0), (2, 0), (0, 1), (0, 2), (3, 0), (2, 1), (0, 3), (1, 1), (3, 1),
+    (2, 2), (0, 4), (1, 2), (1, 3), (2, 3), (1, 4), (3, 3), (2, 4), (3, 4), (3, 2),
 )
 CARRIER = {(0, 4): 0, (1, 4): 0, (2, 4): 0, (3, 4): 0, (1, 0): 0, (2, 0): 1, (3, 0): 0, (3, 1): 0}
 
@@ -40,21 +40,21 @@
 SEM_Y, SEM_X1, SEM_X2, SEM_FAR, SEM_CORE, SEM_SIDE, SEMS = 0, 5, 10, 15, 20, 40, 42
 
 ROW_BLOCKS = ((0, 512), (512, 512), (1024, 512), (1536, 512 + DROWS))
-KEY_BLOCKS = ((0, 256), (256, 256), (512, 512), (1024, 512), (1536, 512), (2048, 256), (2304, 256))
+KEY_BLOCKS = ((0, 256), (256, 256), (512, 512), (1024, 512), (1536, 512), (2048, 512))
 TALL, BROAD, SUB = 512 + DROWS, 512, 256
 
 SERVICE = {
-    (0, 2): (("sum",), ("ready", 2)),
-    (0, 3): (("far", 0),),
-    (1, 0): (("near", 1), ("ready", 3)),
-    (1, 2): (("near", 2),),
-    (2, 0): (("side",), ("sum",), ("ready", 4)),
+    (0, 1): (("ready", 2), ("sum",)),
+    (0, 3): (("ready", 3), ("near", 1), ("far", 0)),
+    (1, 1): (("sum",),),
+    (1, 2): (("ready", 4),),
+    (2, 0): (("near", 2), ("side",)),
     (2, 2): (("near", 3),),
-    (3, 0): (("far", 2), ("sum",)),
-    (3, 2): (("near", 4),),
-    (4, 1): (("far", 3), ("sum",)),
-    (4, 2): (("far", 4),),
-    (6, 0): (("sum",),),
+    (3, 0): (("near", 4), ("sum",)),
+    (3, 2): (("far", 2), ("far", 4)),
+    (4, 0): (("far", 3),),
+    (4, 2): (("sum",),),
+    (5, 0): (("sum",),),
 }
 
 

time: 42.5 us -> 45 us (1.059)
  Pallas kernels: 40.1 us -> 42.8 us
    pallas_call x1, Pallas kernels: 38.8 us -> 41.4 us  [on_device(): pl.pallas_call(fused_kernel, name='attend', in_specs=[smem, smem] + [hbm]...]
where the time goes in v5:
time: 45 us; the launch traced here: 44.9 us
  Pallas kernels  42.8 us (95%)
  between operations  2.09 us (5%)
    pallas_call x1, Pallas kernels, on_device(): pl.pallas_call(fused_kernel, name='attend', in_specs=[smem, smem] + [hbm]...  41.4 us
    pallas_call x1, Pallas kernels, on_device(): pl.pallas_call(write_kernel, name='write', in_specs=[vmem] * 3, out_specs...  1.35 us

profile of v5, /device:TPU:2, one launch (start us, length us, event | category | flops | bytes accessed | tf_op | source)
XLA Modules:
  0.0 44.9 jit_solution(2127714944623583074)
XLA Ops:
  1.9 41.4 %attend.1 = (bf16[2048,512]{1,0:T(8,128)(2,1)S(1)}, bf16[64,512]{1,0:T(8,128)(2,1)S(1)}, bf16[2,576]{1,0:T(2,128)(2,1)S(1)}) custom-call(s32[1]{0:T(128)S(6)} %copy.13.prefix_ref, s32[1]{0:T(128)S(6)} %copy.14.slen_ref, s32[1,32]{1,0:T(1,128)} %hits_hbm.1, bf16[64,576]{1,0:T(8,128)(2,1)} %bitcast.10, bf16[16,576]{1,0:T(8,128)(2,1)} %bitcast.13, ...), custom_call_target="tpu_custom_call" | custom-call | tf_op jit(solution)/shard_map/attend/pallas_call | solution.py:511
  43.4 1.4 %write.1 = (bf16[2048,512]{1,0:T(8,128)(2,1)}, bf16[64,512]{1,0:T(8,128)(2,1)}, bf16[2,576]{1,0:T(2,128)(2,1)}) custom-call(bf16[2048,512]{1,0:T(8,128)(2,1)S(1)} %get-tuple-element.9.out_vmem, bf16[64,512]{1,0:T(8,128)(2,1)S(1)} %get-tuple-element.10.dec_vmem, bf16[2,576]{1,0:T(2,128)(2,1)S(1)} %get-tuple-element.11.fresh_vmem), custom_call_target="tpu_custom_call" | custom-call | tf_op jit(solution)/shard_map/write/pallas_call | solution.py:567
